TPU v7x, 256 devices: a whole 4x4x8 slice. The times are simulated.
256 devices in a mesh: gx: 8 (over y, core), gy: 4 (over x), gz: 8 (over z).
Axes of the slice: x: 4, y: 4, z: 8, core: 2. Of those that a mesh axis runs over, the one named last changes fastest.
Arguments:
- offsets: float32 [3, 524288], P(None, ('gx', 'gy', 'gz')), may hold values from 0 to 1
- anchor: float32 [3, 524288], P(None, ('gx', 'gy', 'gz')), may hold values from 0 to 1
- stiffness: float32 [524288], P(('gx', 'gy', 'gz')), may hold values from 0.02 to 0.2
- lattice_block: int32 [524288, 1], P(('gx', 'gy', 'gz')), may hold values from 0 to 31; in each aligned block of 2048 rows (0 to 2047, 2048 to 4095, ...) at most 128 rows name the same one
- tile_ids: int32 [524288], P(('gx', 'gy', 'gz')), may hold values from 0 to 127
- populations: float32 [19, 64, 64, 1024], P(None, 'gx', 'gy', 'gz'), may hold values from 0 to 0.44, as said below
- visc_class: int32 [64, 64, 1024], P('gx', 'gy', 'gz'), may hold values from 0 to 3
- fluid_mask: int32 [64, 64, 1024], P('gx', 'gy', 'gz'), may hold values 0 or 1
- tau_table: float32 [4], replicated, may hold values from 0.55 to 1.5
Outputs:
- new_populations: float32 [19, 64, 64, 1024], P(None, 'gx', 'gy', 'gz')
- vertex_velocity: float32 [3, 524288], P(None, ('gx', 'gy', 'gz'))
Inputs may be any that keep to these rules, and one draw needn't show every extreme that they name: `lattice_block`: at most 128 vertices of one cell block name the same lattice brick, and in every draw some brick is named by exactly 128 vertices of some block. `populations`: each distribution lies between 0.7 and 1.3 times its lattice weight.
All inputs are finite; a program needn't handle non-finite values. No bound on the sum of `fluid_mask` on one device may be relied on, other than what follows from the above.
Results may differ from a plain program's by a relative error of at most 0.0003.
Values sent between devices are 32-bit elements; how exact they have to be, the bound alone decides.
A program may use at most 128 MiB of HBM per device.

v0:
```python
import jax
import jax.numpy as jnp
from jax import lax
from jax.sharding import PartitionSpec as P

CAP = 128


lattice_velocity = [
    (0, 0, 0),
    (1, 0, 0),
    (-1, 0, 0),
    (0, 1, 0),
    (0, -1, 0),
    (0, 0, 1),
    (0, 0, -1),
    (1, 1, 0),
    (-1, -1, 0),
    (1, -1, 0),
    (-1, 1, 0),
    (1, 0, 1),
    (-1, 0, -1),
    (1, 0, -1),
    (-1, 0, 1),
    (0, 1, 1),
    (0, -1, -1),
    (0, 1, -1),
    (0, -1, 1),
]
lattice_weight = [1.0 / 3.0] + [1.0 / 18.0] * 6 + [1.0 / 36.0] * 12
opposite = [0, 2, 1, 4, 3, 6, 5, 8, 7, 10, 9, 12, 11, 14, 13, 16, 15, 18, 17]
speed_scale = 20.0


def extended_2(cells, sides, width):
    for axis, dim in sides:
        count = lax.axis_size(axis)
        head = lax.slice_in_dim(cells, 0, width, axis=dim)
        tail = lax.slice_in_dim(cells, cells.shape[dim] - width, cells.shape[dim], axis=dim)
        cells = jnp.concatenate(
            [
                lax.ppermute(tail, axis, [(i, (i + 1) % count) for i in range(count)]),
                cells,
                lax.ppermute(head, axis, [((i + 1) % count, i) for i in range(count)]),
            ],
            axis=dim,
        )
    return cells


def tent_weight(distance, radius):
    return jnp.maximum(0.0, 1.0 - jnp.abs(distance) / radius)


def tile_weights(offsets):
    site = jnp.arange(128, dtype=jnp.int32)
    coord_a = (site // 64).astype(jnp.float32)
    coord_b = (site // 32 % 2).astype(jnp.float32)
    coord_c = (site % 32).astype(jnp.float32)
    return (
        tent_weight(2.0 * offsets[0][:, None] - coord_a[None, :], 1.5)
        * tent_weight(2.0 * offsets[1][:, None] - coord_b[None, :], 1.5)
        * tent_weight(32.0 * offsets[2][:, None] - coord_c[None, :], 2.0)
    )


def moment_of(values, axis_pick):
    total = jnp.zeros_like(values[0])
    for index in range(19):
        coefficient = lattice_velocity[index][axis_pick]
        if coefficient != 0:
            total = total + coefficient * values[index]
    return total


def velocity(populations, force_field):
    density = jnp.sum(populations, axis=0)
    return jnp.stack(
        [
            (moment_of(populations, axis_pick) + 0.5 * force_field[axis_pick]) / density
            for axis_pick in range(3)
        ]
    )


def collide(populations, force_field, relax_time, fluid_flag):
    density = jnp.sum(populations, axis=0)
    flow = [
        (moment_of(populations, axis_pick) + 0.5 * force_field[axis_pick]) / density
        for axis_pick in range(3)
    ]
    speed_sq = flow[0] * flow[0] + flow[1] * flow[1] + flow[2] * flow[2]
    work_rate = flow[0] * force_field[0] + flow[1] * force_field[1] + flow[2] * force_field[2]
    inverse = 1.0 / relax_time
    source_gain = 1.0 - 0.5 * inverse
    result = []
    for index in range(19):
        proj_u = jnp.zeros_like(density)
        proj_f = jnp.zeros_like(density)
        for axis_pick in range(3):
            coefficient = lattice_velocity[index][axis_pick]
            if coefficient != 0:
                proj_u = proj_u + coefficient * flow[axis_pick]
                proj_f = proj_f + coefficient * force_field[axis_pick]
        weight = lattice_weight[index]
        equilib = weight * density * (1.0 + 3.0 * proj_u + 4.5 * proj_u * proj_u - 1.5 * speed_sq)
        source = source_gain * weight * (3.0 * (proj_f - work_rate) + 9.0 * proj_u * proj_f)
        collided = populations[index] - (populations[index] - equilib) * inverse + source
        result.append(jnp.where(fluid_flag > 0.5, collided, populations[opposite[index]]))
    return jnp.stack(result)


def stream(extended, width, margin):
    size_x = extended.shape[1] - 2 * width + 2 * margin
    size_y = extended.shape[2] - 2 * width + 2 * margin
    size_z = extended.shape[3] - 2 * width + 2 * margin
    result = []
    for index in range(19):
        shift_x, shift_y, shift_z = lattice_velocity[index]
        start_x = width - margin - shift_x
        start_y = width - margin - shift_y
        start_z = width - margin - shift_z
        result.append(
            extended[
                index,
                start_x : start_x + size_x,
                start_y : start_y + size_y,
                start_z : start_z + size_z,
            ]
        )
    return jnp.stack(result)


def on_device(
    offsets,
    anchor,
    stiffness,
    lattice_block,
    tile_ids,
    populations,
    visc_class,
    fluid_mask,
    tau_table,
):
    along_gy = lax.axis_size("gy")
    along_gz = lax.axis_size("gz")
    groups = along_gy * along_gz
    capacity = CAP
    slots = groups * capacity
    vertex_force = stiffness[None, :] * (anchor - offsets)
    target = lattice_block[:, 0]
    member = (target[:, None] == jnp.arange(groups, dtype=jnp.int32)[None, :]).astype(jnp.int32)
    before = jnp.cumsum(member, axis=0) - member
    slot_index = target * capacity + jnp.sum(before * member, axis=1)
    vertex_rows = jnp.concatenate(
        [offsets, vertex_force, tile_ids[None, :].astype(jnp.float32)], axis=0
    )
    outgoing = jnp.zeros((7, slots), jnp.float32).at[6].set(-1.0).at[:, slot_index].set(vertex_rows)
    arrived = lax.all_to_all(
        outgoing.reshape(7, groups, capacity), ("gy", "gz"), split_axis=1, concat_axis=1, tiled=True
    ).reshape(7, slots)
    brick_x, brick_y, brick_z = (populations.shape[1], populations.shape[2], populations.shape[3])
    tiles_x, tiles_y, tiles_z = (brick_x // 2, brick_y // 2, brick_z // 32)
    tile_count = tiles_x * tiles_y * tiles_z
    weight_rows = tile_weights(arrived[0:3])
    member_tile = (
        arrived[6][None, :] == jnp.arange(tile_count, dtype=jnp.int32).astype(jnp.float32)[:, None]
    ).astype(jnp.float32)
    load_rows = (weight_rows[:, None, :] * arrived[3:6].T[:, :, None]).reshape(slots, 384)
    spread = jnp.dot(member_tile, load_rows, precision=lax.Precision.HIGHEST)
    force_field = (
        spread.reshape(tiles_x, tiles_y, tiles_z, 3, 2, 2, 32)
        .transpose(3, 0, 4, 1, 5, 2, 6)
        .reshape(3, brick_x, brick_y, brick_z)
    )
    relax_time = jnp.zeros(visc_class.shape, jnp.float32)
    for klass in range(tau_table.shape[0]):
        relax_time = relax_time + jnp.where(visc_class == klass, tau_table[klass], 0.0)
    fluid_flag = fluid_mask.astype(jnp.float32)
    current = populations
    for sweep_idx in range(2):
        collided = collide(current, force_field, relax_time, fluid_flag)
        widened = extended_2(collided, (("gx", 1), ("gy", 2), ("gz", 3)), 1)
        current = stream(widened, 1, 0)
    flow_field = velocity(current, force_field)
    flow_tiles = (
        flow_field.reshape(3, tiles_x, 2, tiles_y, 2, tiles_z, 32)
        .transpose(1, 3, 5, 0, 2, 4, 6)
        .reshape(tile_count, 384)
    )
    picked = lax.dot_general(
        member_tile, flow_tiles, (((0,), (0,)), ((), ())), precision=lax.Precision.HIGHEST
    )
    slot_velocity = (
        speed_scale * jnp.sum(picked.reshape(slots, 3, 128) * weight_rows[:, None, :], axis=2)
    ).T
    returned = lax.all_to_all(
        slot_velocity.reshape(3, groups, capacity),
        ("gy", "gz"),
        split_axis=1,
        concat_axis=1,
        tiled=True,
    ).reshape(3, slots)
    vertex_velocity = returned[:, slot_index]
    return (current, vertex_velocity)


def solution(mesh):
    placed = (
        P(None, ("gx", "gy", "gz")),
        P(None, ("gx", "gy", "gz")),
        P(("gx", "gy", "gz")),
        P(("gx", "gy", "gz"), None),
        P(("gx", "gy", "gz")),
        P(None, "gx", "gy", "gz"),
        P("gx", "gy", "gz"),
        P("gx", "gy", "gz"),
        P(),
    )
    return jax.shard_map(
        on_device,
        mesh=mesh,
        in_specs=placed,
        out_specs=(P(None, "gx", "gy", "gz"), P(None, ("gx", "gy", "gz"))),
        check_vma=False,
    )
```

profile of v0, /device:TPU:2, one launch (start us, length us, event | category | flops | bytes accessed | tf_op | source)
XLA Modules:
  0.0 278.9 jit_solution(8275944509600702312)
XLA Ops:
  2.1 9.1 %reduce-window.6 = s32[32,16,128]{2,1,0:T(8,128)S(1)} reduce-window(s32[32,16,128]{2,1,0:T(8,128)S(1)} %fusion.15, s32[]{:T(128)} %constant.136.clone.1), window={size=1x1x128 pad=0_0x0_0x127_0}, to_apply=%region_1.2 | reduce-window | flops 8323072 | bytes 524292 | tf_op jit(solution)/shard_map/reduce-window
  14.1 6.4 %scatter_fusion = f32[7,4096]{0,1:T(8,128)S(1)} fusion(f32[7,4096]{0,1:T(8,128)S(1)} %copy-done.6, s32[2048]{0:T(1024)S(1)} %bitcast.569, f32[2048,7]{1,0:T(8,128)S(1)} %copy.32), kind=kCustom, calls=%fused_computation.1 | custom fusion | bytes 180224 | tf_op jit(solution)/shard_map/scatter | solution.py:158
  21.7 12.3 %all-to-all-start = ((f32[7,32,128]{2,0,1:T(8,128)}), f32[7,32,128]{2,0,1:T(8,128)S(1)}, u32[]{:S(2)}, u32[]{:S(2)}) async-start(f32[7,32,128]{2,0,1:T(8,128)} %copy.33), calls=%async_computation | async-start | bytes 262144 | tf_op jit(solution)/shard_map/all_to_all | solution.py:159
  34.9 8.2 %all-to-all-done = f32[7,32,128]{2,0,1:T(8,128)S(1)} async-done(((f32[7,32,128]{2,0,1:T(8,128)}), f32[7,32,128]{2,0,1:T(8,128)S(1)}, u32[]{:S(2)}, u32[]{:S(2)}) %all-to-all-start) | async-done | bytes 114720 | tf_op jit(solution)/shard_map/all_to_all | solution.py:159
  45.1 7.5 %fusion.5 = f32[3,4,2,8,2,4,32]{6,3,4,2,0,5,1:T(8,128)S(1)} fusion(f32[3,2,2,32,4096,1,1]{4,3,2,1,0,6,5:T(8,128)S(1)} %bitcast.563, f32[4,8,4]{1,2,0:T(4,128)S(1)} %add_convert_fusion, f32[4096]{0:T(1024)S(1)} %bitcast.573), kind=kOutput, calls=%fused_computation.12 | convolution fusion | flops 2416443392 | bytes 6504960 | tf_op jit(solution)/shard_map/dot_general | solution.py:170
  60.5 4.6 %constant_dynamic-update-slice_fusion.18 = (f32[19,8,16,128]{3,2,1,0:T(8,128)S(1)}, f32[8,16,128]{2,1,0:T(8,128)}, f32[8,16,128]{2,1,0:T(8,128)S(1)}, f32[8,16,1...) fusion(f32[]{:T(128)} %bitcast.46, ...), kind=kLoop, calls=%fused_computation.47 | loop fusion | flops 1425407 | bytes 2113552
  65.2 2.5 constant_dynamic-update-slice_fusion.17
  67.7 2.5 constant_dynamic-update-slice_fusion.16
  70.2 2.5 constant_dynamic-update-slice_fusion.15
  72.6 2.5 constant_dynamic-update-slice_fusion.14
  75.1 2.5 constant_dynamic-update-slice_fusion.13
  77.6 2.5 constant_dynamic-update-slice_fusion.12
  80.1 3.1 %constant_dynamic-update-slice_fusion.11 = (f32[19,8,16,128]{3,2,1,0:T(8,128)S(1)}, f32[8,16,128]{2,1,0:T(8,128)}) fusion(f32[19,8,16,128]{3,2,1,0:T(8,128)S(1)} %constant_dynamic-update-slice_fusion.12, pred[8,16,128]{2,1,0:T(8,128)(4,1)S(1)} %get-tuple-element.79, f32[8,16,128]{2,1,0:T(8,128)S(1)} %get-tuple-element.74, ...), kind=kLoop, calls=%fused_computation.40 | loop fusion | flops 589824 | bytes 802832
  83.2 2.5 constant_dynamic-update-slice_fusion.10
  85.7 2.5 constant_dynamic-update-slice_fusion.9
  88.2 2.5 constant_dynamic-update-slice_fusion.8
  90.7 3.1 %constant_dynamic-update-slice_fusion.7 = (f32[19,8,16,128]{3,2,1,0:T(8,128)S(1)}, f32[8,16,128]{2,1,0:T(8,128)}) fusion(f32[19,8,16,128]{3,2,1,0:T(8,128)S(1)} %constant_dynamic-update-slice_fusion.8, pred[8,16,128]{2,1,0:T(8,128)(4,1)S(1)} %get-tuple-element.79, f32[8,16,128]{2,1,0:T(8,128)S(1)} %get-tuple-element.74, ...), kind=kLoop, calls=%fused_computation.36 | loop fusion | flops 589824 | bytes 802832
  93.8 2.5 constant_dynamic-update-slice_fusion.6
  96.3 2.5 constant_dynamic-update-slice_fusion.5
  98.8 2.5 constant_dynamic-update-slice_fusion.4
  101.3 3.1 %constant_dynamic-update-slice_fusion.3 = (f32[19,8,16,128]{3,2,1,0:T(8,128)S(1)}, f32[8,16,128]{2,1,0:T(8,128)}) fusion(f32[19,8,16,128]{3,2,1,0:T(8,128)S(1)} %constant_dynamic-update-slice_fusion.4, pred[8,16,128]{2,1,0:T(8,128)(4,1)S(1)} %get-tuple-element.79, f32[8,16,128]{2,1,0:T(8,128)S(1)} %get-tuple-element.74, ...), kind=kLoop, calls=%fused_computation.32 | loop fusion | flops 589824 | bytes 802832
  104.3 2.5 constant_dynamic-update-slice_fusion.2
  106.8 2.5 constant_dynamic-update-slice_fusion.1
  109.3 2.5 constant_dynamic-update-slice_fusion
  112.9 2.7 collective-permute-done.1
  115.7 3.1 %collective-permute-done = f32[19,1,16,128]{3,2,1,0:T(8,128)S(1)} collective-permute-done((f32[19,1,16,128]{3,2,1,0:T(8,128)S(1)}, f32[19,1,16,128]{3,2,1,0:T(8,128)S(1)}, u32[]{:S(2)}, u32[]{:S(2)}) %collective-permute-start) | collective-permute-done | bytes 155680 | tf_op jit(solution)/shard_map/ppermute | solution.py:42
  121.2 2.6 collective-permute-done.3
  126.2 2.9 %fusion.364 = (f32[19,10,18,1]{3,2,1,0:T(8,128)}, f32[19,10,18,1]{3,2,1,0:T(8,128)}) fusion(f32[19,10,18,128]{3,2,1,0:T(8,128)S(1)} %pad_maximum_fusion), kind=kLoop, calls=%fused_computation.596 | loop fusion | bytes 54720 | tf_op jit(solution)/shard_map/slice | solution.py:38
  129.1 3.5 %copy.43 = f32[19,10,18,1]{0,3,2,1:T(1,128)} copy(f32[19,10,18,1]{3,2,1,0:T(8,128)} %get-tuple-element.82) | data formatting | bytes 27360 | tf_op jit(solution)/shard_map/slice | solution.py:38
  132.9 3.4 %copy.41 = f32[19,10,18,1]{0,3,2,1:T(1,128)} copy(f32[19,10,18,1]{3,2,1,0:T(8,128)} %get-tuple-element.83) | data formatting | bytes 27360 | tf_op jit(solution)/shard_map/slice | solution.py:39
  138.0 3.9 %copy.44 = f32[19,10,18,1]{3,2,1,0:T(8,128)} copy(f32[19,10,18,1]{0,3,2,1:T(1,128)} %collective-permute-done.5) | data formatting | bytes 27360 | tf_op jit(solution)/shard_map/ppermute | solution.py:44
  142.5 3.9 %copy.42 = f32[19,10,18,1]{3,2,1,0:T(8,128)} copy(f32[19,10,18,1]{0,3,2,1:T(1,128)} %collective-permute-done.4) | data formatting | bytes 27360 | tf_op jit(solution)/shard_map/ppermute | solution.py:42
  146.4 5.3 %constant_dynamic-update-slice_fusion.56 = (f32[19,8,16,128]{3,2,1,0:T(8,128)S(1)}, f32[8,16,128]{2,1,0:T(8,128)}, f32[8,16,128]{2,1,0:T(8,128)S(1)}, f32[8,16,1...) fusion(pred[8,16,128]{2,1,0:T(8,128)(4,1)S(1)} %get-tuple-eleme, ...), kind=kLoop, calls=%fused_computation.85 | loop fusion | flops 2834431 | bytes 3826416
  152.7 2.5 constant_dynamic-update-slice_fusion.36
  155.2 2.5 constant_dynamic-update-slice_fusion.35
  157.7 2.5 constant_dynamic-update-slice_fusion.34
  160.2 2.5 constant_dynamic-update-slice_fusion.33
  162.7 2.5 constant_dynamic-update-slice_fusion.32
  165.2 2.5 constant_dynamic-update-slice_fusion.31
  167.7 2.5 constant_dynamic-update-slice_fusion.30
  170.2 2.5 constant_dynamic-update-slice_fusion.29
  172.7 2.5 constant_dynamic-update-slice_fusion.28
  175.2 2.5 constant_dynamic-update-slice_fusion.27
  177.7 2.5 constant_dynamic-update-slice_fusion.26
  180.2 2.5 constant_dynamic-update-slice_fusion.25
  182.7 2.5 constant_dynamic-update-slice_fusion.24
  185.2 2.5 constant_dynamic-update-slice_fusion.23
  187.7 2.5 constant_dynamic-update-slice_fusion.22
  190.2 2.5 constant_dynamic-update-slice_fusion.21
  192.7 2.5 constant_dynamic-update-slice_fusion.20
  195.2 2.5 constant_dynamic-update-slice_fusion.19
  197.8 2.9 %collective-permute-start.7 = (f32[19,1,16,128]{3,2,1,0:T(8,128)S(1)}, f32[19,1,16,128]{3,2,1,0:T(8,128)S(1)}, u32[]{:S(2)}, u32[]{:S(2)}) collective-permute-start(f32[19,1,16,128]{3,2,1,0:T(8,128)S(1)} %get-tuple-element.89), channel_id=1, source_target_pairs={{32,0},{64,32},{96,64},{128,96},{160,128},{192,160},{224,192},{0,2... | collective-permute-start | bytes 466952 | tf_op jit(solution)/shard_map/ppermute | solution.py:44
  200.7 2.9 %collective-permute-done.6 = f32[19,1,16,128]{3,2,1,0:T(8,128)S(1)} collective-permute-done((f32[19,1,16,128]{3,2,1,0:T(8,128)S(1)}, f32[19,1,16,128]{3,2,1,0:T(8,128)S(1)}, u32[]{:S(2)}, u32[]{:S(2)}) %collective-permute-start.6) | collective-permute-done | bytes 155680 | tf_op jit(solution)/shard_map/ppermute | solution.py:42
  210.1 2.9 %fusion.363 = (f32[19,10,18,1]{3,2,1,0:T(8,128)}, f32[19,10,18,1]{3,2,1,0:T(8,128)}) fusion(f32[19,10,18,128]{3,2,1,0:T(8,128)S(1)} %pad_maximum_fusion.1), kind=kLoop, calls=%fused_computation.595 | loop fusion | bytes 54720 | tf_op jit(solution)/shard_map/slice | solution.py:38
  212.9 2.8 %copy.47 = f32[19,10,18,1]{0,3,2,1:T(1,128)S(1)} copy(f32[19,10,18,1]{3,2,1,0:T(8,128)} %get-tuple-element.80) | data formatting | bytes 27360 | tf_op jit(solution)/shard_map/slice | solution.py:38
  215.8 3.4 %copy.45 = f32[19,10,18,1]{0,3,2,1:T(1,128)} copy(f32[19,10,18,1]{3,2,1,0:T(8,128)} %get-tuple-element.81) | data formatting | bytes 27360 | tf_op jit(solution)/shard_map/slice | solution.py:39
  219.6 2.8 %collective-permute-start.11 = (f32[19,10,18,1]{0,3,2,1:T(1,128)S(1)}, f32[19,10,18,1]{0,3,2,1:T(1,128)S(1)}, u32[]{:S(2)}, u32[]{:S(2)}) collective-permute-start(f32[19,10,18,1]{0,3,2,1:T(1,128)S(1)} %copy.47), channel_id=1, source_target_pairs={{1,0},{2,1},{3,2},{4,3},{5,4},{6,5},{7,6},{0,7},{9,8},{10,9},{11,1... | collective-permute-start | bytes 41048 | tf_op jit(solution)/shard_map/ppermute | solution.py:44
  225.3 3.1 %copy.48 = f32[19,10,18,1]{3,2,1,0:T(8,128)} copy(f32[19,10,18,1]{0,3,2,1:T(1,128)S(1)} %collective-permute-done.11) | data formatting | bytes 27360 | tf_op jit(solution)/shard_map/ppermute | solution.py:44
  228.4 4.1 %copy.46 = f32[19,10,18,1]{3,2,1,0:T(8,128)} copy(f32[19,10,18,1]{0,3,2,1:T(1,128)} %collective-permute-done.10) | data formatting | bytes 27360 | tf_op jit(solution)/shard_map/ppermute | solution.py:42
  232.4 2.4 add_divide_fusion.2
  248.0 3.2 %multiply_reduce_fusion = f32[4096,3]{0,1:T(4,128)S(1)} fusion(f32[3,128,128]{2,1,0:T(8,128)S(1)} %bitcast.566, f32[4096,128]{0,1:T(8,128)S(1)} %maximum_multiply_fusion, f32[4096]{0:T(1024)S(1)} %bitcast.574, f32[128]{0:T(128)S(1)} %iota_convert_fusion), kind=kOutput, calls=%fused_computation.2 | convolution fusion | flops 2419576832 | bytes 2359808 | tf_op jit(solution)/shard_map/dot_general | solution.py:191
  251.8 11.0 %all-to-all-start.1 = ((f32[3,32,128]{2,0,1:T(4,128)}), f32[3,32,128]{2,0,1:T(4,128)S(1)}, u32[]{:S(2)}, u32[]{:S(2)}) async-start(f32[3,32,128]{2,0,1:T(4,128)} %multiply_bitcast_fusion), calls=%async_computation.1 | async-start | bytes 131072 | tf_op jit(solution)/shard_map/all_to_all | solution.py:197
  263.5 8.2 %all-to-all-done.1 = f32[3,32,128]{2,0,1:T(4,128)S(1)} async-done(((f32[3,32,128]{2,0,1:T(4,128)}), f32[3,32,128]{2,0,1:T(4,128)S(1)}, u32[]{:S(2)}, u32[]{:S(2)}) %all-to-all-start.1) | async-done | bytes 49184 | tf_op jit(solution)/shard_map/all_to_all | solution.py:197
  272.3 5.5 %gather_fusion = f32[2048,3]{1,0:T(8,128)S(1)} fusion(f32[3,4096]{0,1:T(8,128)S(1)} %bitcast.564, s32[2048]{0:T(1024)S(1)} %broadcast_clamp_fusion), kind=kCustom, calls=%fused_computation | custom fusion | bytes 57344 | tf_op jit(solution)/shard_map/gather | solution.py:204
  (150 shorter events, 51.3 us)
Async XLA Ops:
  0.6 11.2 %copy-start.21 = (s32[2048,1]{0,1:T(1,128)S(1)}, s32[2048,1]{0,1:T(1,128)}, u32[]{:S(2)}) copy-start(s32[2048,1]{0,1:T(1,128)} %param.14) | copy-start | bytes 24580
  1.3 10.7 %copy-start.20 = (f32[3,2048]{1,0:T(4,128)S(1)}, f32[3,2048]{1,0:T(4,128)}, u32[]{:S(2)}) copy-start(f32[3,2048]{1,0:T(4,128)} %param.11) | copy-start | bytes 73732
  1.3 10.7 %copy-start.25 = (f32[3,2048]{1,0:T(4,128)S(1)}, f32[3,2048]{1,0:T(4,128)}, u32[]{:S(2)}) copy-start(f32[3,2048]{1,0:T(4,128)} %param.12) | copy-start | bytes 73732
  1.4 10.7 %copy-start.27 = (f32[2048]{0:T(1024)S(1)}, f32[2048]{0:T(1024)}, u32[]{:S(2)}) copy-start(f32[2048]{0:T(1024)} %param.13) | copy-start | bytes 24580
  12.5 1.6 copy-start.6
  20.4 13.7 %copy-start.3 = (f32[19,8,16,128]{3,2,1,0:T(8,128)S(1)}, f32[19,8,16,128]{3,2,1,0:T(8,128)}, u32[]{:S(2)}) copy-start(f32[19,8,16,128]{3,2,1,0:T(8,128)} %param.16) | copy-start | bytes 3735556
  21.7 12.5 %copy-start.26 = (f32[4]{0:T(128)S(1)}, f32[4]{0:T(128)}, u32[]{:S(2)}) copy-start(f32[4]{0:T(128)} %param.19) | copy-start | bytes 52
  21.7 21.3 %all-to-all-start = ((f32[7,32,128]{2,0,1:T(8,128)}), f32[7,32,128]{2,0,1:T(8,128)S(1)}, u32[]{:S(2)}, u32[]{:S(2)}) async-start(f32[7,32,128]{2,0,1:T(8,128)} %copy.33), calls=%async_computation | async-start | bytes 262144 | tf_op jit(solution)/shard_map/all_to_all | solution.py:159
  43.1 2.0 copy-start.22
  53.6 6.9 %copy-start = (s32[8,16,128]{2,1,0:T(8,128)S(1)}, s32[8,16,128]{2,1,0:T(8,128)}, u32[]{:S(2)}) copy-start(s32[8,16,128]{2,1,0:T(8,128)} %param.17) | copy-start | bytes 196612
  53.6 6.9 %copy-start.24 = (s32[8,16,128]{2,1,0:T(8,128)S(1)}, s32[8,16,128]{2,1,0:T(8,128)}, u32[]{:S(2)}) copy-start(s32[8,16,128]{2,1,0:T(8,128)} %param.18) | copy-start | bytes 196612
  60.5 4.7 %copy-start.4 = (f32[19,8,16,128]{3,2,1,0:T(8,128)S(1)}, f32[19,8,16,128]{3,2,1,0:T(8,128)}, u32[]{:S(2)}) copy-start(f32[19,8,16,128]{3,2,1,0:T(8,128)} %param.16) | copy-start | bytes 3735556
  111.8 13.4 %copy-start.5 = (f32[19,8,16,128]{3,2,1,0:T(8,128)}, f32[19,8,16,128]{3,2,1,0:T(8,128)S(1)}, u32[]{:S(2)}) copy-start(f32[19,8,16,128]{3,2,1,0:T(8,128)S(1)} %constant_dynamic-update-slice_fusion) | copy-start | bytes 3735556
  111.9 3.8 %collective-permute-start.1 = (f32[19,1,16,128]{3,2,1,0:T(8,128)S(1)}, f32[19,1,16,128]{3,2,1,0:T(8,128)S(1)}, u32[]{:S(2)}, u32[]{:S(2)}) collective-permute-start(f32[19,1,16,128]{3,2,1,0:T(8,128)S(1)} %get-tuple-element.90), channel_id=1, source_target_pairs={{32,0},{64,32},{96,64},{128,96},{160,128},{192,160},{224,192},{0,2... | collective-permute-start | bytes 466952 | tf_op jit(solution)/shard_map/ppermute | solution.py:44
  112.9 5.9 %collective-permute-start = (f32[19,1,16,128]{3,2,1,0:T(8,128)S(1)}, f32[19,1,16,128]{3,2,1,0:T(8,128)S(1)}, u32[]{:S(2)}, u32[]{:S(2)}) collective-permute-start(f32[19,1,16,128]{3,2,1,0:T(8,128)S(1)} %get-tuple-element.91), channel_id=1, source_target_pairs={{0,32},{32,64},{64,96},{96,128},{128,160},{160,192},{192,224},{224... | collective-permute-start | bytes 466952 | tf_op jit(solution)/shard_map/ppermute | solution.py:42
  118.9 4.9 %collective-permute-start.3 = (f32[19,10,1,128]{3,2,1,0:T(1,128)S(1)}, f32[19,10,1,128]{3,2,1,0:T(1,128)S(1)}, u32[]{:S(2)}, u32[]{:S(2)}) collective-permute-start(f32[19,10,1,128]{3,2,1,0:T(1,128)S(1)} %get-tuple-element.86), channel_id=1, source_target_pairs={{8,0},{16,8},{24,16},{0,24},{9,1},{17,9},{25,17},{1,25},{10,2},{18... | collective-permute-start | bytes 291848 | tf_op jit(solution)/shard_map/ppermute | solution.py:44
  120.6 4.6 %collective-permute-start.2 = (f32[19,10,1,128]{3,2,1,0:T(1,128)S(1)}, f32[19,10,1,128]{3,2,1,0:T(1,128)S(1)}, u32[]{:S(2)}, u32[]{:S(2)}) collective-permute-start(f32[19,10,1,128]{3,2,1,0:T(1,128)S(1)} %get-tuple-element.87), channel_id=1, source_target_pairs={{0,8},{8,16},{16,24},{24,0},{1,9},{9,17},{17,25},{25,1},{2,10},{10... | collective-permute-start | bytes 291848 | tf_op jit(solution)/shard_map/ppermute | solution.py:42
  123.8 1.4 copy-start.12
  125.2 0.6 copy-start.13
  132.5 5.5 %collective-permute-start.5 = (f32[19,10,18,1]{0,3,2,1:T(1,128)}, f32[19,10,18,1]{0,3,2,1:T(1,128)}, u32[]{:S(2)}, u32[]{:S(2)}) collective-permute-start(f32[19,10,18,1]{0,3,2,1:T(1,128)} %copy.43), channel_id=1, source_target_pairs={{1,0},{2,1},{3,2},{4,3},{5,4},{6,5},{7,6},{0,7},{9,8},{10,9},{11,1... | collective-permute-start | bytes 41048 | tf_op jit(solution)/shard_map/ppermute | solution.py:44
  136.4 6.1 %collective-permute-start.4 = (f32[19,10,18,1]{0,3,2,1:T(1,128)}, f32[19,10,18,1]{0,3,2,1:T(1,128)}, u32[]{:S(2)}, u32[]{:S(2)}) collective-permute-start(f32[19,10,18,1]{0,3,2,1:T(1,128)} %copy.41), channel_id=1, source_target_pairs={{0,1},{1,2},{2,3},{3,4},{4,5},{5,6},{6,7},{7,0},{8,9},{9,10},{10,1... | collective-permute-start | bytes 41048 | tf_op jit(solution)/shard_map/ppermute | solution.py:42
  157.7 10.0 %copy-start.17 = (f32[8,16,128]{2,1,0:T(8,128)S(1)}, f32[8,16,128]{2,1,0:T(8,128)}, u32[]{:S(2)}) copy-start(f32[8,16,128]{2,1,0:T(8,128)} %get-tuple-element.71) | copy-start | bytes 196612
  170.2 7.5 %copy-start.16 = (f32[8,16,128]{2,1,0:T(8,128)S(1)}, f32[8,16,128]{2,1,0:T(8,128)}, u32[]{:S(2)}) copy-start(f32[8,16,128]{2,1,0:T(8,128)} %get-tuple-element.69) | copy-start | bytes 196612
  180.2 7.5 %copy-start.15 = (f32[8,16,128]{2,1,0:T(8,128)S(1)}, f32[8,16,128]{2,1,0:T(8,128)}, u32[]{:S(2)}) copy-start(f32[8,16,128]{2,1,0:T(8,128)} %get-tuple-element.67) | copy-start | bytes 196612
  197.7 11.7 %copy-start.1 = (f32[19,8,16,128]{3,2,1,0:T(8,128)}, f32[19,8,16,128]{3,2,1,0:T(8,128)S(1)}, u32[]{:S(2)}) copy-start(f32[19,8,16,128]{3,2,1,0:T(8,128)S(1)} %constant_dynamic-update-slice_fusion.19) | copy-start | bytes 3735556
  197.7 5.9 %collective-permute-start.6 = (f32[19,1,16,128]{3,2,1,0:T(8,128)S(1)}, f32[19,1,16,128]{3,2,1,0:T(8,128)S(1)}, u32[]{:S(2)}, u32[]{:S(2)}) collective-permute-start(f32[19,1,16,128]{3,2,1,0:T(8,128)S(1)} %get-tuple-element.88), channel_id=1, source_target_pairs={{0,32},{32,64},{64,96},{96,128},{128,160},{160,192},{192,224},{224... | collective-permute-start | bytes 466952 | tf_op jit(solution)/shard_map/ppermute | solution.py:42
  197.8 5.9 %collective-permute-start.7 = (f32[19,1,16,128]{3,2,1,0:T(8,128)S(1)}, f32[19,1,16,128]{3,2,1,0:T(8,128)S(1)}, u32[]{:S(2)}, u32[]{:S(2)}) collective-permute-start(f32[19,1,16,128]{3,2,1,0:T(8,128)S(1)} %get-tuple-element.89), channel_id=1, source_target_pairs={{32,0},{64,32},{96,64},{128,96},{160,128},{192,160},{224,192},{0,2... | collective-permute-start | bytes 466952 | tf_op jit(solution)/shard_map/ppermute | solution.py:44
  203.6 5.8 %copy-start.7 = (f32[19,1,16,128]{3,2,1,0:T(8,128)}, f32[19,1,16,128]{3,2,1,0:T(8,128)S(1)}, u32[]{:S(2)}) copy-start(f32[19,1,16,128]{3,2,1,0:T(8,128)S(1)} %collective-permute-done.6) | copy-start | bytes 466948
  203.6 5.8 %copy-start.8 = (f32[19,1,16,128]{3,2,1,0:T(8,128)}, f32[19,1,16,128]{3,2,1,0:T(8,128)S(1)}, u32[]{:S(2)}) copy-start(f32[19,1,16,128]{3,2,1,0:T(8,128)S(1)} %collective-permute-done.7) | copy-start | bytes 466948
  203.8 5.4 %collective-permute-start.8 = (f32[19,10,1,128]{3,2,1,0:T(1,128)S(1)}, f32[19,10,1,128]{3,2,1,0:T(1,128)S(1)}, u32[]{:S(2)}, u32[]{:S(2)}) collective-permute-start(f32[19,10,1,128]{3,2,1,0:T(1,128)S(1)} %get-tuple-element.84), channel_id=1, source_target_pairs={{0,8},{8,16},{16,24},{24,0},{1,9},{9,17},{17,25},{25,1},{2,10},{10... | collective-permute-start | bytes 291848 | tf_op jit(solution)/shard_map/ppermute | solution.py:42
  204.5 4.9 %collective-permute-start.9 = (f32[19,10,1,128]{3,2,1,0:T(1,128)S(1)}, f32[19,10,1,128]{3,2,1,0:T(1,128)S(1)}, u32[]{:S(2)}, u32[]{:S(2)}) collective-permute-start(f32[19,10,1,128]{3,2,1,0:T(1,128)S(1)} %get-tuple-element.85), channel_id=1, source_target_pairs={{8,0},{16,8},{24,16},{0,24},{9,1},{17,9},{25,17},{1,25},{10,2},{18... | collective-permute-start | bytes 291848 | tf_op jit(solution)/shard_map/ppermute | solution.py:44
  209.2 0.6 copy-start.9
  209.4 0.6 copy-start.11
  219.2 9.2 %collective-permute-start.10 = (f32[19,10,18,1]{0,3,2,1:T(1,128)}, f32[19,10,18,1]{0,3,2,1:T(1,128)}, u32[]{:S(2)}, u32[]{:S(2)}) collective-permute-start(f32[19,10,18,1]{0,3,2,1:T(1,128)} %copy.45), channel_id=1, source_target_pairs={{0,1},{1,2},{2,3},{3,4},{4,5},{5,6},{6,7},{7,0},{8,9},{9,10},{10,1... | collective-permute-start | bytes 41048 | tf_op jit(solution)/shard_map/ppermute | solution.py:42
  219.6 5.7 %collective-permute-start.11 = (f32[19,10,18,1]{0,3,2,1:T(1,128)S(1)}, f32[19,10,18,1]{0,3,2,1:T(1,128)S(1)}, u32[]{:S(2)}, u32[]{:S(2)}) collective-permute-start(f32[19,10,18,1]{0,3,2,1:T(1,128)S(1)} %copy.47), channel_id=1, source_target_pairs={{1,0},{2,1},{3,2},{4,3},{5,4},{6,5},{7,6},{0,7},{9,8},{10,9},{11,1... | collective-permute-start | bytes 41048 | tf_op jit(solution)/shard_map/ppermute | solution.py:44
  228.4 4.1 %copy-start.2 = (f32[19,8,16,128]{3,2,1,0:T(8,128)S(1)}, f32[19,8,16,128]{3,2,1,0:T(8,128)}, u32[]{:S(2)}) copy-start(f32[19,8,16,128]{3,2,1,0:T(8,128)} %copy-done.1) | copy-start | bytes 3735556
  228.4 4.1 %copy-start.10 = (f32[19,10,1,128]{3,2,1,0:T(1,128)S(1)}, f32[19,10,1,128]{3,2,1,0:T(1,128)}, u32[]{:S(2)}) copy-start(f32[19,10,1,128]{3,2,1,0:T(1,128)} %copy-done.9) | copy-start | bytes 291844
  234.9 10.8 %copy-start.18 = (f32[1,8,16,128]{3,2,1,0:T(8,128)S(1)}, f32[1,8,16,128]{3,2,1,0:T(8,128)}, u32[]{:S(2)}) copy-start(f32[1,8,16,128]{3,2,1,0:T(8,128)} %mul.1965) | copy-start | bytes 196612
  234.9 10.8 %copy-start.19 = (f32[1,8,16,128]{3,2,1,0:T(8,128)S(1)}, f32[1,8,16,128]{3,2,1,0:T(8,128)}, u32[]{:S(2)}) copy-start(f32[1,8,16,128]{3,2,1,0:T(8,128)} %mul.1970) | copy-start | bytes 196612
  244.4 1.7 copy-start.14
  246.7 1.2 copy-start.23
  251.8 19.8 %all-to-all-start.1 = ((f32[3,32,128]{2,0,1:T(4,128)}), f32[3,32,128]{2,0,1:T(4,128)S(1)}, u32[]{:S(2)}, u32[]{:S(2)}) async-start(f32[3,32,128]{2,0,1:T(4,128)} %multiply_bitcast_fusion), calls=%async_computation.1 | async-start | bytes 131072 | tf_op jit(solution)/shard_map/all_to_all | solution.py:197
where the time goes:
time: 284 us; the launch traced here: 279 us
  other arithmetic  120 us (42%)
  local copies, waits for them, and re-layouts  76.5 us (27%)
  starting transfers between devices  38 us (13%)
  waiting for transfers between devices  32.2 us (11%)
  matrix products  10.8 us (4%)
    unnamed x36, other arithmetic  96.4 us
    unnamed x75, local copies, waits for them, and re-layouts  15.3 us
    all_to_all x1, starting transfers between devices, on_device(): lax.all_to_all(outgoing.reshape(7, groups, capacity), ('gy', 'gz'), split...  12.3 us
    slice x5, local copies, waits for them, and re-layouts, extended_2(): head = lax.slice_in_dim(cells, 0, width, axis=dim)  12 us
    ppermute x6, starting transfers between devices, extended_2(): lax.ppermute(head, axis, [((i + 1) % count, i) for i in range(count)])  11.3 us
    all_to_all x1, starting transfers between devices, on_device(): lax.all_to_all(slot_velocity.reshape(3, groups, capacity), ('gy', 'gz'),...  11 us
    ppermute x6, waiting for transfers between devices, extended_2(): lax.ppermute(tail, axis, [(i, (i + 1) % count) for i in range(count)])  10.3 us
    another operation x3, other arithmetic  9.41 us
  transfers between devices with their start and end apart: 14, of which 10 were waited for; matrix products, arithmetic and copies ran while one was open for 5% of the time, Pallas kernels for 0%

commit v1 on v0

v1 whole, which is shorter than its diff:
```python
import functools

import jax
import jax.numpy as jnp
from jax import lax
from jax.experimental import pallas as pl
from jax.experimental.pallas import tpu as pltpu
from jax.sharding import PartitionSpec as P

MESH = pl.DeviceIdType.MESH
CAP = 128
BX, BY, BZ = 8, 16, 128
SITES = BX * BY
XPAD, YPAD = BX + 2, 32
F32, BF16, I32 = jnp.float32, jnp.bfloat16, jnp.int32

lattice_velocity = [
    (0, 0, 0),
    (1, 0, 0),
    (-1, 0, 0),
    (0, 1, 0),
    (0, -1, 0),
    (0, 0, 1),
    (0, 0, -1),
    (1, 1, 0),
    (-1, -1, 0),
    (1, -1, 0),
    (-1, 1, 0),
    (1, 0, 1),
    (-1, 0, -1),
    (1, 0, -1),
    (-1, 0, 1),
    (0, 1, 1),
    (0, -1, -1),
    (0, 1, -1),
    (0, -1, 1),
]
lattice_weight = [1.0 / 3.0] + [1.0 / 18.0] * 6 + [1.0 / 36.0] * 12
speed_scale = 20.0
pairs = [(i, i + 1) for i in range(1, 19, 2)]


def crossing(axis, sign):
    return [i for i in range(19) if lattice_velocity[i][axis] == sign]


XSET = [crossing(0, 1), crossing(0, -1)]
YSET = [crossing(1, 1), crossing(1, -1)]
ZSET = [crossing(2, 1), crossing(2, -1)]


def dist_of(*velocity):
    return lattice_velocity.index(tuple(velocity))


def z_lane(side, index, x):
    return ZSET[side].index(index) * XPAD + x + 1


def row_of(index, x, y):
    return (index * XPAD + x + 1) * YPAD + 8 + y


def moments(f, force):
    density = functools.reduce(lambda a, b: a + b, f)
    inverse = 1.0 / density
    flow = []
    for axis in range(3):
        plus = [f[i] for i in crossing(axis, 1)]
        minus = [f[i] for i in crossing(axis, -1)]
        total = functools.reduce(lambda a, b: a + b, plus) - functools.reduce(lambda a, b: a + b, minus)
        flow.append((total + 0.5 * force[axis]) * inverse)
    return density, flow


def collide(f, force, omega, fluid):
    density, flow = moments(f, force)
    speed_sq = flow[0] * flow[0] + flow[1] * flow[1] + flow[2] * flow[2]
    work = flow[0] * force[0] + flow[1] * force[1] + flow[2] * force[2]
    gain = 1.0 - 0.5 * omega
    keep = 1.0 - omega
    amount = omega * density
    base = amount * (1.0 - 1.5 * speed_sq) - (3.0 * gain) * work
    momentum = [amount * flow[a] for a in range(3)]
    push = [gain * force[a] for a in range(3)]
    steep = [4.5 * momentum[a] + 9.0 * push[a] for a in range(3)]
    slope = [3.0 * (momentum[a] + push[a]) for a in range(3)]
    result = [None] * 19
    result[0] = jnp.where(fluid, keep * f[0] + lattice_weight[0] * base, f[0])

    def along(values, velocity):
        total = None
        for axis in range(3):
            if velocity[axis]:
                if total is None:
                    total = values[axis] if velocity[axis] > 0 else -values[axis]
                else:
                    total = total + values[axis] if velocity[axis] > 0 else total - values[axis]
        return total

    for i, j in pairs:
        velocity = lattice_velocity[i]
        even = base + along(flow, velocity) * along(steep, velocity)
        odd = along(slope, velocity)
        weight = lattice_weight[i]
        result[i] = jnp.where(fluid, keep * f[i] + weight * (even + odd), f[j])
        result[j] = jnp.where(fluid, keep * f[j] + weight * (even - odd), f[i])
    return result


def kernel(
    sizes,
    off_ref,
    anc_ref,
    stf_ref,
    tgt_ref,
    tid_ref,
    tau_ref,
    pop_hbm,
    cls_hbm,
    flu_hbm,
    out_hbm,
    vel_ref,
    pops,
    cls,
    flu,
    rows,
    rt,
    lhs,
    outbuf,
    inbuf,
    wz,
    wxy,
    load,
    acc,
    force,
    field,
    xs,
    xr,
    ys,
    yr,
    xyr,
    zs,
    zr,
    xzr,
    yzr,
    zp,
    ubuf,
    newp,
    vbuf,
    ret,
    in_sem,
    out_sem,
    fwd_send,
    fwd_recv,
    halo_send,
    halo_recv,
    back_send,
    back_recv,
):
    n_gx, n_gy, n_gz = sizes
    groups = n_gy * n_gz
    verts = off_ref.shape[1]
    chunks = verts // 128
    gx, gy, gz = lax.axis_index("gx"), lax.axis_index("gy"), lax.axis_index("gz")

    def device(dx, dy, dz):
        return (
            lax.rem(gx + dx + n_gx, n_gx),
            lax.rem(gy + dy + n_gy, n_gy),
            lax.rem(gz + dz + n_gz, n_gz),
        )

    loads = [
        pltpu.make_async_copy(pop_hbm, pops, in_sem.at[0]),
        pltpu.make_async_copy(cls_hbm, cls, in_sem.at[1]),
        pltpu.make_async_copy(flu_hbm, flu, in_sem.at[2]),
    ]
    for copy in loads:
        copy.start()

    barrier = pltpu.get_barrier_semaphore()

    @pl.loop(1, groups)
    def _(d):
        pl.semaphore_signal(
            barrier, inc=1, device_id=device(0, d // n_gz, lax.rem(d, n_gz)), device_id_type=MESH
        )

    others = [(sx, 0, 0) for sx in (1, -1)]
    others += [(sx, sy, 0) for sx in (1, -1) for sy in (1, -1)]
    others += [(sx, 0, sz) for sx in (1, -1) for sz in (1, -1)]
    for offset in others:
        pl.semaphore_signal(barrier, inc=1, device_id=device(*offset), device_id_type=MESH)

    target = tgt_ref[...]
    rel_y = lax.rem(target // n_gz - gy + n_gy, n_gy)
    rel_z = lax.rem(lax.rem(target, n_gz) - gz + n_gz, n_gz)
    rel = rel_y * n_gz + rel_z
    member = rel == lax.broadcasted_iota(I32, (groups, verts), 0)
    member_f = jnp.where(member, 1.0, 0.0).astype(F32)
    stacked = jnp.concatenate([member_f[:, c * 128 : (c + 1) * 128] for c in range(chunks)], axis=0)
    row_id = lax.broadcasted_iota(I32, (128, 256), 0)
    col_id = lax.broadcasted_iota(I32, (128, 256), 1)
    prefix = jnp.where((row_id < col_id) | (col_id >= 128), 1.0, 0.0).astype(BF16)
    counts = jnp.dot(stacked.astype(BF16), prefix, preferred_element_type=F32)
    base = jnp.zeros((groups, 128), F32)
    slot_id = lax.broadcasted_iota(I32, (128, 128), 0).astype(F32)
    for c in range(chunks):
        part = counts[c * groups : (c + 1) * groups]
        rank = jnp.sum(
            member_f[:, c * 128 : (c + 1) * 128] * (part[:, :128] + base), axis=0, keepdims=True
        )
        base = base + part[:, 128:]
        rt[:, c * 128 : (c + 1) * 128] = jnp.where(rank == slot_id, 1.0, 0.0).astype(BF16)

    def high(value):
        return value.astype(BF16).astype(F32)

    offs = off_ref[...]
    push = stf_ref[...] * (anc_ref[...] - offs)
    offs_hi = high(offs)
    offs_mid = high(offs - offs_hi)
    push_hi = high(push)
    rows[...] = jnp.zeros((16, verts), F32)
    rows[0:3, :] = offs_hi
    rows[3:6, :] = push_hi
    rows[6:7, :] = tid_ref[...].astype(F32)
    rows[7:8, :] = (offs - offs_hi - offs_mid)[2:3]
    rows[8:11, :] = offs_mid
    rows[11:14, :] = push - push_hi
    for d in range(groups):
        lhs[d * 16 : (d + 1) * 16, :] = jnp.where(rel == d, rows[...], 0.0).astype(BF16)
    packed = lax.dot_general(
        lhs[...], rt[...], (((1,), (1,)), ((), ())), preferred_element_type=F32
    )
    sub8 = lax.broadcasted_iota(I32, (8, 128), 0)
    lane8 = lax.broadcasted_iota(I32, (8, 128), 1)
    for d in range(groups):
        both = packed[d * 16 : d * 16 + 8] + packed[d * 16 + 8 : d * 16 + 16]
        fine = pltpu.roll(both, 3, axis=0)
        outbuf[d] = both + jnp.where(sub8 == 2, fine, 0.0)
    inbuf[0] = outbuf[0]

    pl.semaphore_wait(barrier, groups - 1 + len(others))

    def forward(d):
        return pltpu.make_async_remote_copy(
            src_ref=outbuf.at[d],
            dst_ref=inbuf.at[d],
            send_sem=fwd_send.at[d],
            recv_sem=fwd_recv.at[d],
            device_id=device(0, d // n_gz, lax.rem(d, n_gz)),
            device_id_type=MESH,
        )

    @pl.loop(1, groups)
    def _(d):
        forward(d).start()

    x_id = lax.broadcasted_iota(I32, (BX, 128), 0)
    y_id = lax.broadcasted_iota(I32, (BY, 128), 0)
    z_id = lax.broadcasted_iota(I32, (BZ, 128), 0)
    z_half = 0.5 * z_id.astype(F32)

    def spread(d):
        blk = inbuf[d]
        tile = blk[6:7].astype(I32)
        tile_x, tile_y, tile_z = tile // 32, lax.rem(tile // 4, 8), lax.rem(tile, 4)
        dist_x = 2.0 * blk[0:1] - (x_id - 2 * tile_x).astype(F32)
        wx = jnp.where(x_id // 2 == tile_x, jnp.maximum(0.0, 1.0 - jnp.abs(dist_x) * (1.0 / 1.5)), 0.0)
        dist_y = 2.0 * blk[1:2] - (y_id - 2 * tile_y).astype(F32)
        wy = jnp.where(y_id // 2 == tile_y, jnp.maximum(0.0, 1.0 - jnp.abs(dist_y) * (1.0 / 1.5)), 0.0)
        place = 16.0 * blk[2:3] + 16.0 * tile_z.astype(F32)
        weight = jnp.where(z_id // 32 == tile_z, jnp.maximum(0.0, 1.0 - jnp.abs(place - z_half)), 0.0)
        lanes = pl.ds(pl.multiple_of(d * 128, 128), 128)
        weight_hi = weight.astype(BF16)
        wz[0:BZ, lanes] = weight_hi
        wz[BZ : 2 * BZ, lanes] = (weight - weight_hi.astype(F32)).astype(BF16)
        for x in range(BX):
            plane = wx[x : x + 1] * wy
            wxy[x * BY : (x + 1) * BY, lanes] = plane
            for c in range(3):
                value = plane * blk[3 + c : 4 + c]
                value_hi = value.astype(BF16)
                at = c * SITES + x * BY
                load[at : at + BY, lanes] = value_hi
                at += 3 * SITES
                load[at : at + BY, lanes] = (value - value_hi.astype(F32)).astype(BF16)

    per = 8
    for part in range(groups // per):

        @pl.loop(part * per, (part + 1) * per)
        def _(d):
            @pl.when(d > 0)
            def _():
                forward(d).wait_recv()

            spread(d)

        span = slice(part * per * 128, (part + 1) * per * 128)
        product = lax.dot_general(
            load[:, span], wz[:, span], (((1,), (1,)), ((), ())), preferred_element_type=F32
        )
        if part == 0:
            acc[...] = product
        else:
            acc[...] += product
    half = 3 * SITES
    force[...] = (acc[0:half, 0:128] + acc[0:half, 128:256]) + (
        acc[half : 2 * half, 0:128] + acc[half : 2 * half, 128:256]
    )

    for copy in loads:
        copy.wait()

    taus = [1.0 / jnp.full((8, 128), tau_ref[k], F32) for k in range(4)]

    def site_values(x, h):
        rows_at = pl.ds(8 * h, 8)
        klass = cls[x, rows_at, :]
        omega = jnp.where(
            klass < 2, jnp.where(klass == 0, taus[0], taus[1]), jnp.where(klass == 2, taus[2], taus[3])
        )
        return omega, flu[x, rows_at, :] > 0

    def forces(x, h):
        return [
            force[pl.ds(pl.multiple_of(c * SITES + x * BY + 8 * h, 8), 8), :] for c in range(3)
        ]

    def messages(p):
        found = []
        for s, sign in enumerate((1, -1)):
            found.append(((sign, 0, 0), xs.at[p, s], xr.at[p, s]))
            found.append(((0, sign, 0), ys.at[p, s], yr.at[p, s]))
            found.append(((0, 0, sign), zs.at[p, s], zr.at[p, s]))
            for t, other in enumerate((1, -1)):
                spot = YSET[s].index(dist_of(other, sign, 0))
                found.append(((other, sign, 0), ys.at[p, s, spot], xyr.at[p, s, t]))
                found.append(((other, 0, sign), zs.at[p, s], xzr.at[p, s, t]))
                edge = pl.ds(8 if other > 0 else 0, 8)
                found.append(((0, other, sign), zs.at[p, s, edge], yzr.at[p, s, t]))
        return found

    def halo(p):
        return [
            pltpu.make_async_remote_copy(
                src_ref=src,
                dst_ref=dst,
                send_sem=halo_send.at[p, m],
                recv_sem=halo_recv.at[p, m],
                device_id=device(*offset),
                device_id_type=MESH,
            )
            for m, (offset, src, dst) in enumerate(messages(p))
        ]

    def streamed(p, x, h):
        found = []
        for i in range(19):
            cx, cy, cz = lattice_velocity[i]
            start = row_of(i, x - cx, 8 * h - cy)
            if cy == 0:
                start = pl.multiple_of(start, 8)
            value = field[p, pl.ds(start, 8), :]
            if cz:
                s = 0 if cz > 0 else 1
                border = zp[p, s, 8 + 8 * h - cy : 16 + 8 * h - cy, :]
                lane = z_lane(s, i, x - cx)
                edge = 0 if cz > 0 else 127
                shift = 128 - lane if cz > 0 else 127 - lane
                value = jnp.where(
                    lane8 == edge,
                    pltpu.roll(border, shift, axis=1),
                    pltpu.roll(value, 1 if cz > 0 else 127, axis=1),
                )
            found.append(value)
        return found

    def sweep(p, source):
        def body(x, borders):
            borders = list(borders)
            for h in range(2):
                omega, fluid = site_values(x, h)
                result = collide(source(x, h), forces(x, h), omega, fluid)
                for i in range(19):
                    field[p, pl.ds(pl.multiple_of(row_of(i, x, 8 * h), 8), 8), :] = result[i]
                for s in range(2):
                    for i in ZSET[s]:
                        lane = z_lane(s, i, x)
                        shift = lane + 1 if s == 0 else lane
                        borders[2 * s + h] = jnp.where(
                            lane8 == lane, pltpu.roll(result[i], shift, axis=1), borders[2 * s + h]
                        )
            return tuple(borders)

        zero = jnp.zeros((8, 128), F32)
        borders = lax.fori_loop(0, BX, body, (zero, zero, zero, zero))
        for s in range(2):
            for h in range(2):
                zs[p, s, 8 * h : 8 * h + 8, :] = borders[2 * s + h]
            for k, i in enumerate(YSET[s]):
                ys[p, s, k] = field[p, pl.ds(row_of(i, 0, BY - 1 if s == 0 else 0), BX, stride=YPAD), :]
            for k, i in enumerate(XSET[s]):
                start = row_of(i, BX - 1 if s == 0 else 0, 0)
                xs[p, s, k] = field[p, start : start + BY, :]
        copies = halo(p)
        for copy in copies:
            copy.start()
        for copy in copies:
            copy.wait_recv()
        lane16 = lax.broadcasted_iota(I32, (BY, 128), 1)
        for s, sign in enumerate((1, -1)):
            for k, i in enumerate(XSET[s]):
                start = row_of(i, -1 if s == 0 else BX, 0)
                field[p, start : start + BY, :] = xr[p, s, k]
            for k, i in enumerate(YSET[s]):
                field[p, pl.ds(row_of(i, 0, -1 if s == 0 else BY), BX, stride=YPAD), :] = yr[p, s, k]
            plane = zr[p, s]
            for t, other in enumerate((1, -1)):
                i = dist_of(other, sign, 0)
                start = row_of(i, -1 if other > 0 else BX, -1 if s == 0 else BY)
                row = BX - 1 if other > 0 else 0
                field[p, start : start + 1, :] = xyr[p, s, t, row : row + 1, :]
                i = dist_of(other, 0, sign)
                lane = z_lane(s, i, -1 if other > 0 else BX)
                shift = 128 - BX if other > 0 else BX
                plane = jnp.where(lane16 == lane, pltpu.roll(xzr[p, s, t], shift, axis=1), plane)
                to, row = (7, 7) if other > 0 else (24, 0)
                zp[p, s, to : to + 1, :] = yzr[p, s, t, row : row + 1, :]
            zp[p, s, 8:24, :] = plane
        return copies

    def first(x, h):
        return [pops[i, x, pl.ds(8 * h, 8), :] for i in range(19)]

    sent = sweep(0, first)
    sent += sweep(1, functools.partial(streamed, 0))

    @pl.loop(0, BX)
    def _(x):
        for h in range(2):
            result = streamed(1, x, h)
            for i in range(19):
                newp[i, x, pl.ds(8 * h, 8), :] = result[i]
            density, flow = moments(result, forces(x, h))
            for c in range(3):
                ubuf[pl.ds(pl.multiple_of(c * SITES + x * BY + 8 * h, 8), 8), :] = flow[c]

    store = pltpu.make_async_copy(newp, out_hbm, out_sem)
    store.start()

    flow = ubuf[...]
    flow_hi = flow.astype(BF16)
    flow_lo = (flow - flow_hi.astype(F32)).astype(BF16)
    flow_all = jnp.concatenate([flow_hi, flow_hi, flow_lo, flow_lo], axis=1)

    def backward(d):
        return pltpu.make_async_remote_copy(
            src_ref=vbuf.at[pl.ds(pl.multiple_of(d * 8, 8), 8)],
            dst_ref=ret.at[pl.ds(pl.multiple_of(d * 8, 8), 8)],
            send_sem=back_send.at[d],
            recv_sem=back_recv.at[d],
            device_id=device(0, -(d // n_gz), -lax.rem(d, n_gz)),
            device_id_type=MESH,
        )

    @pl.loop(0, groups // 2)
    def _(pair):
        lanes = pl.ds(pl.multiple_of(pair * 256, 256), 256)
        block = wz[:, lanes]
        picked = jnp.dot(
            flow_all, jnp.concatenate([block, block], axis=0), preferred_element_type=F32
        )
        plane = wxy[:, lanes]
        for c in range(3):
            speed = speed_scale * jnp.sum(
                picked[c * SITES : (c + 1) * SITES] * plane, axis=0, keepdims=True
            )
            for e in range(2):
                vbuf[pl.ds(pair * 16 + 8 * e + c, 1), :] = speed[:, e * 128 : (e + 1) * 128]
        for e in range(2):
            d = pair * 2 + e

            @pl.when(d > 0)
            def _():
                backward(d).start()

    ret[0:8, :] = vbuf[0:8, :]

    @pl.loop(1, groups)
    def _(d):
        backward(d).wait_recv()

    answer = jnp.concatenate([ret[pl.ds(c, groups, stride=8), :] for c in range(3)], axis=0)
    answer_hi = answer.astype(BF16)
    answer_lo = (answer - answer_hi.astype(F32)).astype(BF16)
    found = jnp.dot(
        jnp.concatenate([answer_hi, answer_lo], axis=0), rt[...], preferred_element_type=F32
    )
    found = found[0 : 3 * groups] + found[3 * groups :]
    for c in range(3):
        vel_ref[c : c + 1, :] = jnp.sum(
            jnp.where(member, found[c * groups : (c + 1) * groups], 0.0), axis=0, keepdims=True
        )

    for copy in sent:
        copy.wait_send()

    @pl.loop(1, groups)
    def _(d):
        forward(d).wait_send()
        backward(d).wait_send()

    store.wait()


def on_device(
    sizes,
    offsets,
    anchor,
    stiffness,
    lattice_block,
    tile_ids,
    populations,
    visc_class,
    fluid_mask,
    tau_table,
):
    groups = sizes[1] * sizes[2]
    verts = offsets.shape[1]
    vmem = pl.BlockSpec(memory_space=pltpu.VMEM)
    smem = pl.BlockSpec(memory_space=pltpu.SMEM)
    hbm = pl.BlockSpec(memory_space=pl.ANY)
    return pl.pallas_call(
        functools.partial(kernel, sizes),
        out_shape=(
            jax.ShapeDtypeStruct(populations.shape, F32),
            jax.ShapeDtypeStruct((3, verts), F32),
        ),
        in_specs=[vmem] * 5 + [smem] + [hbm] * 3,
        out_specs=(hbm, vmem),
        scratch_shapes=[
            pltpu.VMEM((19, BX, BY, BZ), F32),
            pltpu.VMEM((BX, BY, BZ), I32),
            pltpu.VMEM((BX, BY, BZ), I32),
            pltpu.VMEM((16, verts), F32),
            pltpu.VMEM((CAP, verts), BF16),
            pltpu.VMEM((groups * 16, verts), BF16),
            pltpu.VMEM((groups, 8, CAP), F32),
            pltpu.VMEM((groups, 8, CAP), F32),
            pltpu.VMEM((2 * BZ, groups * CAP), BF16),
            pltpu.VMEM((SITES, groups * CAP), F32),
            pltpu.VMEM((6 * SITES, groups * CAP), BF16),
            pltpu.VMEM((6 * SITES, 2 * BZ), F32),
            pltpu.VMEM((3 * SITES, BZ), F32),
            pltpu.VMEM((2, 19 * XPAD * YPAD, BZ), F32),
            pltpu.VMEM((2, 2, 5, BY, BZ), F32),
            pltpu.VMEM((2, 2, 5, BY, BZ), F32),
            pltpu.VMEM((2, 2, 5, BX, BZ), F32),
            pltpu.VMEM((2, 2, 5, BX, BZ), F32),
            pltpu.VMEM((2, 2, 2, BX, BZ), F32),
            pltpu.VMEM((2, 2, BY, 128), F32),
            pltpu.VMEM((2, 2, BY, 128), F32),
            pltpu.VMEM((2, 2, 2, BY, 128), F32),
            pltpu.VMEM((2, 2, 2, 8, 128), F32),
            pltpu.VMEM((2, 2, YPAD, 128), F32),
            pltpu.VMEM((3 * SITES, BZ), F32),
            pltpu.VMEM((19, BX, BY, BZ), F32),
            pltpu.VMEM((groups * 8, CAP), F32),
            pltpu.VMEM((groups * 8, CAP), F32),
            pltpu.SemaphoreType.DMA((3,)),
            pltpu.SemaphoreType.DMA,
            pltpu.SemaphoreType.DMA((groups,)),
            pltpu.SemaphoreType.DMA((groups,)),
            pltpu.SemaphoreType.DMA((2, 18)),
            pltpu.SemaphoreType.DMA((2, 18)),
            pltpu.SemaphoreType.DMA((groups,)),
            pltpu.SemaphoreType.DMA((groups,)),
        ],
        compiler_params=pltpu.CompilerParams(
            collective_id=0, has_side_effects=True, vmem_limit_bytes=48 * 1024 * 1024
        ),
    )(
        offsets,
        anchor,
        stiffness.reshape(1, verts),
        lattice_block.reshape(1, verts),
        tile_ids.reshape(1, verts),
        tau_table,
        populations,
        visc_class,
        fluid_mask,
    )


def solution(mesh):
    placed = (
        P(None, ("gx", "gy", "gz")),
        P(None, ("gx", "gy", "gz")),
        P(("gx", "gy", "gz")),
        P(("gx", "gy", "gz"), None),
        P(("gx", "gy", "gz")),
        P(None, "gx", "gy", "gz"),
        P("gx", "gy", "gz"),
        P("gx", "gy", "gz"),
        P(),
    )
    sizes = tuple(mesh.shape[axis] for axis in ("gx", "gy", "gz"))
    return jax.shard_map(
        functools.partial(on_device, sizes),
        mesh=mesh,
        in_specs=placed,
        out_specs=(P(None, "gx", "gy", "gz"), P(None, ("gx", "gy", "gz"))),
        check_vma=False,
    )
```

time: 284 us -> 58.7 us (0.21)
  the two profiles are of different devices: /device:TPU:2 before, /device:TPU:1 now
where the time goes in v1:
time: 58.7 us; the launch traced here: 58.2 us
  Pallas kernels  48.7 us (83%)
  local copies, waits for them, and re-layouts  8.87 us (15%)
  between operations  0.66 us (1%)
    pallas_call x1, Pallas kernels, on_device(): pl.pallas_call(functools.partial(kernel, sizes), out_shape=(jax.ShapeDtyp...  48.7 us
    unnamed x20, local copies, waits for them, and re-layouts  8.87 us

profile of v1, /device:TPU:1, one launch (start us, length us, event | category | flops | bytes accessed | tf_op | source)
XLA Modules:
  0.0 58.2 jit_solution(2647020170890082275)
XLA Ops:
  0.6 0.0 copy-start
  0.6 1.3 %copy-done = f32[19,8,16,128]{3,2,1,0:T(8,128)S(1)} copy-done((f32[19,8,16,128]{3,2,1,0:T(8,128)S(1)}, f32[19,8,16,128]{3,2,1,0:T(8,128)}, u32[]{:S(2)}) %copy-start) | copy-done | bytes 1245208
  1.9 0.0 copy-start.1
  1.9 0.8 %copy-done.1 = s32[8,16,128]{2,1,0:T(8,128)S(1)} copy-done((s32[8,16,128]{2,1,0:T(8,128)S(1)}, s32[8,16,128]{2,1,0:T(8,128)}, u32[]{:S(2)}) %copy-start.1) | copy-done | bytes 65560
  2.8 0.0 copy-start.2
  2.8 0.8 %copy-done.2 = s32[8,16,128]{2,1,0:T(8,128)S(1)} copy-done((s32[8,16,128]{2,1,0:T(8,128)S(1)}, s32[8,16,128]{2,1,0:T(8,128)}, u32[]{:S(2)}) %copy-start.2) | copy-done | bytes 65560
  3.6 0.0 copy-start.3
  3.6 0.8 %copy-done.3 = f32[3,2048]{1,0:T(4,128)S(1)} copy-done((f32[3,2048]{1,0:T(4,128)S(1)}, f32[3,2048]{1,0:T(4,128)}, u32[]{:S(2)}) %copy-start.3) | copy-done | bytes 24600
  4.4 0.0 copy-start.4
  4.4 0.8 %copy-done.4 = f32[3,2048]{1,0:T(4,128)S(1)} copy-done((f32[3,2048]{1,0:T(4,128)S(1)}, f32[3,2048]{1,0:T(4,128)}, u32[]{:S(2)}) %copy-start.4) | copy-done | bytes 24600
  5.1 0.0 copy-start.5
  5.1 0.7 %copy-done.5 = f32[2048]{0:T(1024)S(1)} copy-done((f32[2048]{0:T(1024)S(1)}, f32[2048]{0:T(1024)}, u32[]{:S(2)}) %copy-start.5) | copy-done | bytes 8216
  5.8 0.0 copy-start.6
  5.8 0.7 %copy-done.6 = s32[2048,1]{0,1:T(1,128)S(1)} copy-done((s32[2048,1]{0,1:T(1,128)S(1)}, s32[2048,1]{0,1:T(1,128)}, u32[]{:S(2)}) %copy-start.6) | copy-done | bytes 8216
  6.5 0.0 copy-start.7
  6.5 0.7 %copy-done.7 = s32[2048]{0:T(1024)S(1)} copy-done((s32[2048]{0:T(1024)S(1)}, s32[2048]{0:T(1024)}, u32[]{:S(2)}) %copy-start.7) | copy-done | bytes 8216
  7.2 0.0 copy-start.8
  7.2 0.7 %copy-done.8 = f32[4]{0:T(128)S(1)} copy-done((f32[4]{0:T(128)S(1)}, f32[4]{0:T(128)}, u32[]{:S(2)}) %copy-start.8) | copy-done | bytes 40
  7.9 48.7 %shard_map.104 = (f32[19,8,16,128]{3,2,1,0:T(8,128)S(1)}, f32[3,2048]{1,0:T(4,128)S(1)}) custom-call(f32[3,2048]{1,0:T(4,128)S(1)} %copy-done.3, f32[3,2048]{1,0:T(4,128)S(1)} %copy-done.4, f32[1,2048]{1,0:T(1,128)S(1)} %bitcast.3, s32[1,2048]{1,0:T(1,128)S(1)} %bitcast.4, s32[1,2048]{1,0:T(1,128)S(1)} %bitcast.5, f32[4]{0:T(128)S(1)} %copy-done.8, ...), custom_call_target="tpu_custom_call" | custom-call | tf_op jit(solution)/shard_map/pallas_call | solution.py:537
  56.6 1.0 %copy.13 = f32[19,8,16,128]{3,2,1,0:T(8,128)} copy(f32[19,8,16,128]{3,2,1,0:T(8,128)S(1)} %get-tuple-element.4) | data formatting | bytes 2490368
  57.6 0.6 %copy.14 = f32[3,2048]{1,0:T(4,128)} copy(f32[3,2048]{1,0:T(4,128)S(1)} %get-tuple-element.5) | data formatting | bytes 49152
Async XLA Ops:
  0.6 1.3 %copy-start = (f32[19,8,16,128]{3,2,1,0:T(8,128)S(1)}, f32[19,8,16,128]{3,2,1,0:T(8,128)}, u32[]{:S(2)}) copy-start(f32[19,8,16,128]{3,2,1,0:T(8,128)} %pop_hbm.1) | copy-start | bytes 3735556
  1.9 0.8 %copy-start.1 = (s32[8,16,128]{2,1,0:T(8,128)S(1)}, s32[8,16,128]{2,1,0:T(8,128)}, u32[]{:S(2)}) copy-start(s32[8,16,128]{2,1,0:T(8,128)} %cls_hbm.1) | copy-start | bytes 196612
  2.8 0.8 %copy-start.2 = (s32[8,16,128]{2,1,0:T(8,128)S(1)}, s32[8,16,128]{2,1,0:T(8,128)}, u32[]{:S(2)}) copy-start(s32[8,16,128]{2,1,0:T(8,128)} %flu_hbm.1) | copy-start | bytes 196612
  3.6 0.8 %copy-start.3 = (f32[3,2048]{1,0:T(4,128)S(1)}, f32[3,2048]{1,0:T(4,128)}, u32[]{:S(2)}) copy-start(f32[3,2048]{1,0:T(4,128)} %off_ref.1) | copy-start | bytes 73732
  4.4 0.8 %copy-start.4 = (f32[3,2048]{1,0:T(4,128)S(1)}, f32[3,2048]{1,0:T(4,128)}, u32[]{:S(2)}) copy-start(f32[3,2048]{1,0:T(4,128)} %anc_ref.1) | copy-start | bytes 73732
  5.1 0.7 %copy-start.5 = (f32[2048]{0:T(1024)S(1)}, f32[2048]{0:T(1024)}, u32[]{:S(2)}) copy-start(f32[2048]{0:T(1024)} %param.11) | copy-start | bytes 24580
  5.8 0.7 %copy-start.6 = (s32[2048,1]{0,1:T(1,128)S(1)}, s32[2048,1]{0,1:T(1,128)}, u32[]{:S(2)}) copy-start(s32[2048,1]{0,1:T(1,128)} %param.12) | copy-start | bytes 24580
  6.5 0.7 %copy-start.7 = (s32[2048]{0:T(1024)S(1)}, s32[2048]{0:T(1024)}, u32[]{:S(2)}) copy-start(s32[2048]{0:T(1024)} %param.13) | copy-start | bytes 24580
  7.2 0.7 %copy-start.8 = (f32[4]{0:T(128)S(1)}, f32[4]{0:T(128)}, u32[]{:S(2)}) copy-start(f32[4]{0:T(128)} %tau_ref.1) | copy-start | bytes 52

commit v2 on v1

v2 whole, which is shorter than its diff:
```python
import functools

import jax
import jax.numpy as jnp
from jax import lax
from jax.experimental import pallas as pl
from jax.experimental.pallas import tpu as pltpu
from jax.sharding import PartitionSpec as P

MESH = pl.DeviceIdType.MESH
CAP = 128
BX, BY, BZ = 8, 16, 128
SITES = BX * BY
TZ = 32
WIDE = 4
PIECES = [pl.ds(start, min(5, 19 - start)) for start in range(0, 19, 5)]
PARTS = (8, 8, 8, 4, 4)
XPAD, YPAD = BX + 2, 32
F32, BF16, I32 = jnp.float32, jnp.bfloat16, jnp.int32

lattice_velocity = [
    (0, 0, 0),
    (1, 0, 0),
    (-1, 0, 0),
    (0, 1, 0),
    (0, -1, 0),
    (0, 0, 1),
    (0, 0, -1),
    (1, 1, 0),
    (-1, -1, 0),
    (1, -1, 0),
    (-1, 1, 0),
    (1, 0, 1),
    (-1, 0, -1),
    (1, 0, -1),
    (-1, 0, 1),
    (0, 1, 1),
    (0, -1, -1),
    (0, 1, -1),
    (0, -1, 1),
]
lattice_weight = [1.0 / 3.0] + [1.0 / 18.0] * 6 + [1.0 / 36.0] * 12
speed_scale = 20.0
pairs = [(i, i + 1) for i in range(1, 19, 2)]


def crossing(axis, sign):
    return [i for i in range(19) if lattice_velocity[i][axis] == sign]


XSET = [crossing(0, 1), crossing(0, -1)]
YSET = [crossing(1, 1), crossing(1, -1)]
ZSET = [crossing(2, 1), crossing(2, -1)]


def dist_of(*velocity):
    return lattice_velocity.index(tuple(velocity))


def z_lane(side, index, x):
    return ZSET[side].index(index) * XPAD + x + 1


def row_of(index, x, y):
    return (index * XPAD + x + 1) * YPAD + 8 + y


def moments(f, force):
    density = functools.reduce(lambda a, b: a + b, f)
    inverse = 1.0 / density
    flow = []
    for axis in range(3):
        plus = [f[i] for i in crossing(axis, 1)]
        minus = [f[i] for i in crossing(axis, -1)]
        total = functools.reduce(lambda a, b: a + b, plus) - functools.reduce(lambda a, b: a + b, minus)
        flow.append((total + 0.5 * force[axis]) * inverse)
    return density, flow


def collide(f, force, omega, fluid):
    density, flow = moments(f, force)
    speed_sq = flow[0] * flow[0] + flow[1] * flow[1] + flow[2] * flow[2]
    work = flow[0] * force[0] + flow[1] * force[1] + flow[2] * force[2]
    gain = 1.0 - 0.5 * omega
    keep = 1.0 - omega
    amount = omega * density
    base = amount * (1.0 - 1.5 * speed_sq) - (3.0 * gain) * work
    momentum = [amount * flow[a] for a in range(3)]
    push = [gain * force[a] for a in range(3)]
    steep = [4.5 * momentum[a] + 9.0 * push[a] for a in range(3)]
    slope = [3.0 * (momentum[a] + push[a]) for a in range(3)]
    result = [None] * 19
    result[0] = jnp.where(fluid, keep * f[0] + lattice_weight[0] * base, f[0])

    def along(values, velocity):
        total = None
        for axis in range(3):
            if velocity[axis]:
                if total is None:
                    total = values[axis] if velocity[axis] > 0 else -values[axis]
                else:
                    total = total + values[axis] if velocity[axis] > 0 else total - values[axis]
        return total

    for i, j in pairs:
        velocity = lattice_velocity[i]
        even = base + along(flow, velocity) * along(steep, velocity)
        odd = along(slope, velocity)
        weight = lattice_weight[i]
        result[i] = jnp.where(fluid, keep * f[i] + weight * (even + odd), f[j])
        result[j] = jnp.where(fluid, keep * f[j] + weight * (even - odd), f[i])
    return result


def kernel(
    sizes,
    off_hbm,
    anc_hbm,
    stf_hbm,
    tgt_hbm,
    tid_hbm,
    tau_hbm,
    pop_hbm,
    cls_hbm,
    flu_hbm,
    out_hbm,
    vel_ref,
    off_ref,
    anc_ref,
    stf_ref,
    tgt_ref,
    tid_ref,
    tau_ref,
    pops,
    cls,
    flu,
    rows,
    rt,
    lhs,
    outbuf,
    inbuf,
    wz,
    wxy,
    load,
    acc,
    force,
    field0,
    field1,
    xs,
    xr,
    ys,
    yr,
    xyr,
    zs,
    ze,
    zr,
    xzr,
    yzr,
    zp,
    ubuf,
    newp,
    vbuf,
    ret,
    in_sem,
    out_sem,
    fwd_send,
    fwd_recv,
    halo_send,
    halo_recv,
    back_send,
    back_recv,
):
    n_gx, n_gy, n_gz = sizes
    field = (field0, field1)
    groups = n_gy * n_gz
    verts = off_ref.shape[1]
    chunks = verts // 128
    gx, gy, gz = lax.axis_index("gx"), lax.axis_index("gy"), lax.axis_index("gz")

    def device(dx, dy, dz):
        return (
            lax.rem(gx + dx + n_gx, n_gx),
            lax.rem(gy + dy + n_gy, n_gy),
            lax.rem(gz + dz + n_gz, n_gz),
        )

    arguments = [
        (tgt_hbm, tgt_ref),
        (off_hbm, off_ref),
        (anc_hbm, anc_ref),
        (stf_hbm, stf_ref),
        (tid_hbm, tid_ref),
        (tau_hbm, tau_ref),
        (cls_hbm, cls),
        (flu_hbm, flu),
        (pop_hbm, pops),
    ]
    ring = sorted(
        ((dy, dz) for dy in range(n_gy) for dz in range(n_gz)),
        key=lambda at: (min(at[0], n_gy - at[0]) + min(at[1], n_gz - at[1]), at),
    )
    loads = [pltpu.make_async_copy(src, dst, in_sem.at[k]) for k, (src, dst) in enumerate(arguments)]
    for copy in loads:
        copy.start()

    barrier = pltpu.get_barrier_semaphore()

    @pl.loop(1, groups)
    def _(d):
        pl.semaphore_signal(
            barrier, inc=1, device_id=device(0, d // n_gz, lax.rem(d, n_gz)), device_id_type=MESH
        )

    others = [(sx, 0, 0) for sx in (1, -1)]
    others += [(sx, sy, 0) for sx in (1, -1) for sy in (1, -1)]
    others += [(sx, 0, sz) for sx in (1, -1) for sz in (1, -1)]
    for offset in others:
        pl.semaphore_signal(barrier, inc=1, device_id=device(*offset), device_id_type=MESH)

    loads[0].wait()
    target = tgt_ref[...]
    rel_y = lax.rem(target // n_gz - gy + n_gy, n_gy)
    rel_z = lax.rem(lax.rem(target, n_gz) - gz + n_gz, n_gz)
    rel = rel_y * n_gz + rel_z
    member = rel == lax.broadcasted_iota(I32, (groups, verts), 0)
    member_f = jnp.where(member, 1.0, 0.0).astype(F32)
    stacked = jnp.concatenate([member_f[:, c * 128 : (c + 1) * 128] for c in range(chunks)], axis=0)
    row_id = lax.broadcasted_iota(I32, (128, 256), 0)
    col_id = lax.broadcasted_iota(I32, (128, 256), 1)
    prefix = jnp.where((row_id < col_id) | (col_id >= 128), 1.0, 0.0).astype(BF16)
    counts = jnp.dot(stacked.astype(BF16), prefix, preferred_element_type=F32)
    base = jnp.zeros((groups, 128), F32)
    slot_id = lax.broadcasted_iota(I32, (128, 128), 0).astype(F32)
    for c in range(chunks):
        part = counts[c * groups : (c + 1) * groups]
        rank = jnp.sum(
            member_f[:, c * 128 : (c + 1) * 128] * (part[:, :128] + base), axis=0, keepdims=True
        )
        base = base + part[:, 128:]
        rt[:, c * 128 : (c + 1) * 128] = jnp.where(rank == slot_id, 1.0, 0.0).astype(BF16)

    def high(value):
        return value.astype(BF16).astype(F32)

    for copy in loads[1:5]:
        copy.wait()
    offs = off_ref[...]
    push = stf_ref[...] * (anc_ref[...] - offs)
    offs_hi = high(offs)
    offs_mid = high(offs - offs_hi)
    push_hi = high(push)
    rows[...] = jnp.zeros((16, verts), F32)
    rows[0:3, :] = offs_hi
    rows[3:6, :] = push_hi
    rows[6:7, :] = tid_ref[...].astype(F32)
    rows[7:8, :] = (offs - offs_hi - offs_mid)[2:3]
    rows[8:11, :] = offs_mid
    rows[11:14, :] = push - push_hi
    for d in range(groups):
        lhs[d * 16 : (d + 1) * 16, :] = jnp.where(rel == d, rows[...], 0.0).astype(BF16)
    packed = lax.dot_general(
        lhs[...], rt[...], (((1,), (1,)), ((), ())), preferred_element_type=F32
    )
    sub8 = lax.broadcasted_iota(I32, (8, 128), 0)
    lane8 = lax.broadcasted_iota(I32, (8, 128), 1)
    for d in range(groups):
        both = packed[d * 16 : d * 16 + 8] + packed[d * 16 + 8 : d * 16 + 16]
        fine = pltpu.roll(both, 3, axis=0)
        outbuf[d] = both + jnp.where(sub8 == 2, fine, 0.0)
    inbuf[0] = outbuf[0]

    pl.semaphore_wait(barrier, groups - 1 + len(others))

    def forward(k, dy=0, dz=1):
        return pltpu.make_async_remote_copy(
            src_ref=outbuf.at[dy * n_gz + dz],
            dst_ref=inbuf.at[k],
            send_sem=fwd_send.at[k],
            recv_sem=fwd_recv.at[k],
            device_id=device(0, dy, dz),
            device_id_type=MESH,
        )

    for k in range(groups - 1, 0, -1):
        forward(k, *ring[k]).start()

    wide = 128 * WIDE
    x_id = lax.broadcasted_iota(I32, (BX, wide), 0)
    y_id = lax.broadcasted_iota(I32, (BY, wide), 0)
    z_half = 0.5 * lax.broadcasted_iota(I32, (TZ, wide), 0).astype(F32)
    third = 1.0 / 1.5

    def split(value):
        top = value.astype(BF16)
        return top, (value - top.astype(F32)).astype(BF16)

    def spread(at):
        blk = jnp.concatenate([inbuf[at * WIDE + e] for e in range(WIDE)], axis=1)
        tile = blk[6:7].astype(I32)
        tile_x, tile_y, tile_z = tile // 32, lax.rem(tile // 4, 8), lax.rem(tile, 4)
        dist_x = 2.0 * blk[0:1] - lax.rem(x_id, 2).astype(F32)
        wx = jnp.where(x_id // 2 == tile_x, jnp.maximum(0.0, 1.0 - jnp.abs(dist_x) * third), 0.0)
        dist_y = 2.0 * blk[1:2] - lax.rem(y_id, 2).astype(F32)
        wy = jnp.where(y_id // 2 == tile_y, jnp.maximum(0.0, 1.0 - jnp.abs(dist_y) * third), 0.0)
        weight = jnp.maximum(0.0, 1.0 - jnp.abs(16.0 * blk[2:3] - z_half))
        lanes = pl.ds(pl.multiple_of(at * wide, wide), wide)
        wz[:, lanes] = weight
        for x in range(BX):
            for part, value in enumerate(split(wx[x : x + 1] * wy)):
                row = part * SITES + x * BY
                wxy[row : row + BY, lanes] = value
        for c in range(3):
            for part, value in enumerate(split(weight * blk[3 + c : 4 + c])):
                for z in range(BZ // TZ):
                    row = (part * 3 + c) * BZ + z * TZ
                    load[row : row + TZ, lanes] = jnp.where(
                        jnp.broadcast_to(tile_z == z, (TZ, wide)), value, jnp.zeros_like(value)
                    )

    first_slot = 0
    for count in PARTS:

        @pl.loop(max(first_slot, 1), first_slot + count)
        def _(k):
            forward(k).wait_recv()

        @pl.loop(first_slot // WIDE, (first_slot + count) // WIDE)
        def _(at):
            spread(at)

        span = slice(first_slot * 128, (first_slot + count) * 128)
        product = lax.dot_general(
            wxy[:, span], load[:, span], (((1,), (1,)), ((), ())), preferred_element_type=F32
        )
        if first_slot == 0:
            acc[...] = product
        else:
            acc[...] += product
        first_slot += count
    for c in range(3):
        here, there = slice(c * BZ, (c + 1) * BZ), slice((3 + c) * BZ, (4 + c) * BZ)
        force[c * SITES : (c + 1) * SITES, :] = (acc[0:SITES, here] + acc[0:SITES, there]) + (
            acc[SITES:, here] + acc[SITES:, there]
        )

    for copy in loads[5:]:
        copy.wait()

    taus = [1.0 / jnp.full((8, 128), tau_ref[k], F32) for k in range(4)]

    def site_values(x, h):
        rows_at = slice(8 * h, 8 * h + 8)
        klass = cls[x, rows_at, :]
        omega = jnp.where(
            klass < 2, jnp.where(klass == 0, taus[0], taus[1]), jnp.where(klass == 2, taus[2], taus[3])
        )
        return omega, flu[x, rows_at, :] > 0

    def forces(x, h):
        starts = [c * SITES + x * BY + 8 * h for c in range(3)]
        return [force[start : start + 8, :] for start in starts]

    def messages(p):
        early, late = [], []
        for s, sign in enumerate((1, -1)):
            early.append(((sign, 0, 0), xs.at[p, s], xr.at[p, s]))
            late.append(((0, sign, 0), ys.at[p, s], yr.at[p, s]))
            late.append(((0, 0, sign), zs.at[p, s], zr.at[p, s]))
            for t, other in enumerate((1, -1)):
                edge = pl.ds(8 if other > 0 else 0, 8)
                spot = XSET[s].index(dist_of(sign, other, 0))
                early.append(((sign, other, 0), xs.at[p, s, spot, edge], xyr.at[p, s, t]))
                early.append(((other, 0, sign), ze.at[p, s], xzr.at[p, s, t]))
                late.append(((0, other, sign), zs.at[p, s, edge], yzr.at[p, s, t]))
        hops = lambda message: -sum(abs(v) for v in message[0])
        return sorted(early, key=hops), sorted(late, key=hops)

    def halo(p):
        early, late = messages(p)
        return [
            pltpu.make_async_remote_copy(
                src_ref=src,
                dst_ref=dst,
                send_sem=halo_send.at[p, m],
                recv_sem=halo_recv.at[p, m],
                device_id=device(*offset),
                device_id_type=MESH,
            )
            for m, (offset, src, dst) in enumerate(early + late)
        ], len(early)

    def streamed(p, x, h):
        found = []
        for i in range(19):
            cx, cy, cz = lattice_velocity[i]
            start = row_of(i, x - cx, 8 * h - cy)
            value = field[p][start : start + 8, :]
            if cz:
                s = 0 if cz > 0 else 1
                border = zp[p, s, 8 + 8 * h - cy : 16 + 8 * h - cy, :]
                lane = z_lane(s, i, x - cx)
                edge = 0 if cz > 0 else 127
                shift = 128 - lane if cz > 0 else 127 - lane
                value = jnp.where(
                    lane8 == edge,
                    pltpu.roll(border, shift, axis=1),
                    pltpu.roll(value, 1 if cz > 0 else 127, axis=1),
                )
            found.append(value)
        return found

    def sweep(p, source, earlier):
        def plane(x, borders):
            incoming = [source(x, h) for h in range(2)]
            for h in range(2):
                omega, fluid = site_values(x, h)
                result = collide(incoming[h], forces(x, h), omega, fluid)
                for i in range(19):
                    start = row_of(i, x, 8 * h)
                    field[p][start : start + 8, :] = result[i]
                for s in range(2):
                    for i in ZSET[s]:
                        lane = z_lane(s, i, x)
                        shift = lane + 1 if s == 0 else lane
                        borders[2 * s + h] = jnp.where(
                            lane8 == lane, pltpu.roll(result[i], shift, axis=1), borders[2 * s + h]
                        )

        copies, early = halo(p)
        borders = [jnp.zeros((8, 128), F32)] * 4
        for x in (0, BX - 1):
            plane(x, borders)
        for s in range(2):
            for h in range(2):
                ze[p, s, 8 * h : 8 * h + 8, :] = borders[2 * s + h]
            for k, i in enumerate(XSET[s]):
                start = row_of(i, BX - 1 if s == 0 else 0, 0)
                xs[p, s, k] = field[p][start : start + BY, :]
        for copy in copies[:early]:
            copy.start()
        for x in range(1, BX - 1):
            plane(x, borders)
        for s in range(2):
            for h in range(2):
                zs[p, s, 8 * h : 8 * h + 8, :] = borders[2 * s + h]
            for k, i in enumerate(YSET[s]):
                ys[p, s, k] = field[p][pl.ds(row_of(i, 0, BY - 1 if s == 0 else 0), BX, stride=YPAD), :]
        for copy in copies[early:]:
            copy.start()
        earlier()
        for copy in copies:
            copy.wait_recv()
        lane16 = lax.broadcasted_iota(I32, (BY, 128), 1)
        for s, sign in enumerate((1, -1)):
            for k, i in enumerate(XSET[s]):
                start = row_of(i, -1 if s == 0 else BX, 0)
                field[p][start : start + BY, :] = xr[p, s, k]
            for k, i in enumerate(YSET[s]):
                field[p][pl.ds(row_of(i, 0, -1 if s == 0 else BY), BX, stride=YPAD), :] = yr[p, s, k]
            plane = zr[p, s]
            for t, other in enumerate((1, -1)):
                to, row = (-1, 7) if other > 0 else (BY, 0)
                start = row_of(dist_of(sign, other, 0), -1 if s == 0 else BX, to)
                field[p][start : start + 1, :] = xyr[p, s, t, row : row + 1, :]
                zp[p, s, 8 + to : 9 + to, :] = yzr[p, s, t, row : row + 1, :]
                i = dist_of(other, 0, sign)
                lane = z_lane(s, i, -1 if other > 0 else BX)
                shift = 128 - BX if other > 0 else BX
                plane = jnp.where(lane16 == lane, pltpu.roll(xzr[p, s, t], shift, axis=1), plane)
            zp[p, s, 8:24, :] = plane
        return copies

    def first(x, h):
        return [pops[i, x, 8 * h : 8 * h + 8, :] for i in range(19)]

    def forward_sent():
        @pl.loop(1, groups)
        def _(k):
            forward(k).wait_send()

    def halo_sent(copies):
        for copy in copies:
            copy.wait_send()

    sent = sweep(0, first, forward_sent)
    sent = sweep(1, functools.partial(streamed, 0), functools.partial(halo_sent, sent))

    for x in range(BX):
        incoming = [streamed(1, x, h) for h in range(2)]
        for h in range(2):
            for i in range(19):
                newp[i, x, 8 * h : 8 * h + 8, :] = incoming[h][i]
            density, flow = moments(incoming[h], forces(x, h))
            for c in range(3):
                start = c * SITES + x * BY + 8 * h
                ubuf[start : start + 8, :] = flow[c]

    store = pltpu.make_async_copy(newp, out_hbm, out_sem)
    store.start()

    turned = [[], []]
    for c in range(3):
        for part, value in enumerate(split(ubuf[c * SITES : (c + 1) * SITES, :].T)):
            turned[part].append(value)
    flow_hi, flow_lo = (jnp.concatenate(part, axis=0) for part in turned)
    flow_all = jnp.concatenate([flow_hi, flow_hi, flow_lo, flow_lo], axis=1)

    def backward(k, dy=0, dz=1):
        return pltpu.make_async_remote_copy(
            src_ref=vbuf.at[k],
            dst_ref=ret.at[dy * n_gz + dz],
            send_sem=back_send.at[k],
            recv_sem=back_recv.at[k],
            device_id=device(0, -dy, -dz),
            device_id_type=MESH,
        )

    for pair in range(groups // 2 - 1, -1, -1):
        lanes = slice(pair * 256, (pair + 1) * 256)
        block = wxy[:, lanes]
        picked = jnp.dot(
            flow_all, jnp.concatenate([block, block], axis=0), preferred_element_type=F32
        )
        weight = wz[:, lanes]
        tile = jnp.concatenate([inbuf[2 * pair + e, 6:7, :] for e in range(2)], axis=1)
        tile_z = jnp.broadcast_to(lax.rem(tile.astype(I32), 4), (TZ, 256))
        for c in range(3):
            speed = picked[c * BZ : c * BZ + TZ]
            for z in range(1, BZ // TZ):
                at = c * BZ + z * TZ
                speed = jnp.where(tile_z == z, picked[at : at + TZ], speed)
            speed = speed_scale * jnp.sum(speed * weight, axis=0, keepdims=True)
            for e in range(2):
                vbuf[2 * pair + e, c : c + 1, :] = speed[:, e * 128 : (e + 1) * 128]
        for k in (2 * pair + 1, 2 * pair):
            if k > 0:
                backward(k, *ring[k]).start()

    halo_sent(sent)
    ret[0] = vbuf[0]

    @pl.loop(1, groups)
    def _(k):
        backward(k).wait_recv()

    answer = jnp.concatenate([ret[:, c, :] for c in range(3)], axis=0)
    answer_hi = answer.astype(BF16)
    answer_lo = (answer - answer_hi.astype(F32)).astype(BF16)
    found = jnp.dot(
        jnp.concatenate([answer_hi, answer_lo], axis=0), rt[...], preferred_element_type=F32
    )
    found = found[0 : 3 * groups] + found[3 * groups :]
    for c in range(3):
        vel_ref[c : c + 1, :] = jnp.sum(
            jnp.where(member, found[c * groups : (c + 1) * groups], 0.0), axis=0, keepdims=True
        )

    @pl.loop(1, groups)
    def _(k):
        backward(k).wait_send()

    store.wait()


def hand_over(new_hbm, vel_hbm, new_out, vel_out, new_ref, vel_ref, sems):
    hops = [(vel_hbm, vel_ref, vel_out)]
    hops += [(new_hbm.at[part], new_ref.at[part], new_out.at[part]) for part in PIECES]
    inward = [pltpu.make_async_copy(src, mid, sems.at[0, k]) for k, (src, mid, _) in enumerate(hops)]
    outward = [pltpu.make_async_copy(mid, dst, sems.at[1, k]) for k, (_, mid, dst) in enumerate(hops)]
    for copy in inward:
        copy.start()
    for k, copy in enumerate(inward):
        copy.wait()
        outward[k].start()
    for copy in outward:
        copy.wait()


def on_device(
    sizes,
    offsets,
    anchor,
    stiffness,
    lattice_block,
    tile_ids,
    populations,
    visc_class,
    fluid_mask,
    tau_table,
):
    groups = sizes[1] * sizes[2]
    verts = offsets.shape[1]
    vmem = pl.BlockSpec(memory_space=pltpu.VMEM)
    hbm = pl.BlockSpec(memory_space=pltpu.HBM)
    results = pl.pallas_call(
        functools.partial(kernel, sizes),
        out_shape=(
            jax.ShapeDtypeStruct(populations.shape, F32),
            jax.ShapeDtypeStruct((3, verts), F32),
        ),
        in_specs=[hbm] * 9,
        out_specs=(hbm, vmem),
        scratch_shapes=[
            pltpu.VMEM((3, verts), F32),
            pltpu.VMEM((3, verts), F32),
            pltpu.VMEM((1, verts), F32),
            pltpu.VMEM((1, verts), I32),
            pltpu.VMEM((1, verts), I32),
            pltpu.SMEM((4,), F32),
            pltpu.VMEM((19, BX, BY, BZ), F32),
            pltpu.VMEM((BX, BY, BZ), I32),
            pltpu.VMEM((BX, BY, BZ), I32),
            pltpu.VMEM((16, verts), F32),
            pltpu.VMEM((CAP, verts), BF16),
            pltpu.VMEM((groups * 16, verts), BF16),
            pltpu.VMEM((groups, 8, CAP), F32),
            pltpu.VMEM((groups, 8, CAP), F32),
            pltpu.VMEM((TZ, groups * CAP), F32),
            pltpu.VMEM((2 * SITES, groups * CAP), BF16),
            pltpu.VMEM((6 * BZ, groups * CAP), BF16),
            pltpu.VMEM((2 * SITES, 6 * BZ), F32),
            pltpu.VMEM((3 * SITES, BZ), F32),
            pltpu.VMEM((19 * XPAD * YPAD, BZ), F32),
            pltpu.VMEM((19 * XPAD * YPAD, BZ), F32),
            pltpu.VMEM((2, 2, 5, BY, BZ), F32),
            pltpu.VMEM((2, 2, 5, BY, BZ), F32),
            pltpu.VMEM((2, 2, 5, BX, BZ), F32),
            pltpu.VMEM((2, 2, 5, BX, BZ), F32),
            pltpu.VMEM((2, 2, 2, BX, BZ), F32),
            pltpu.VMEM((2, 2, BY, 128), F32),
            pltpu.VMEM((2, 2, BY, 128), F32),
            pltpu.VMEM((2, 2, BY, 128), F32),
            pltpu.VMEM((2, 2, 2, BY, 128), F32),
            pltpu.VMEM((2, 2, 2, 8, 128), F32),
            pltpu.VMEM((2, 2, YPAD, 128), F32),
            pltpu.VMEM((3 * SITES, BZ), F32),
            pltpu.VMEM((19, BX, BY, BZ), F32),
            pltpu.VMEM((groups, 4, CAP), F32),
            pltpu.VMEM((groups, 4, CAP), F32),
            pltpu.SemaphoreType.DMA((9,)),
            pltpu.SemaphoreType.DMA,
            pltpu.SemaphoreType.DMA((groups,)),
            pltpu.SemaphoreType.DMA((groups,)),
            pltpu.SemaphoreType.DMA((2, 18)),
            pltpu.SemaphoreType.DMA((2, 18)),
            pltpu.SemaphoreType.DMA((groups,)),
            pltpu.SemaphoreType.DMA((groups,)),
        ],
        compiler_params=pltpu.CompilerParams(
            collective_id=0, has_side_effects=True, vmem_limit_bytes=60 * 1024 * 1024
        ),
    )(
        offsets,
        anchor,
        stiffness.reshape(1, verts),
        lattice_block.reshape(1, verts),
        tile_ids.reshape(1, verts),
        tau_table,
        populations,
        visc_class,
        fluid_mask,
    )
    return pl.pallas_call(
        hand_over,
        out_shape=[jax.ShapeDtypeStruct(result.shape, F32) for result in results],
        in_specs=[hbm] * 2,
        out_specs=[hbm] * 2,
        scratch_shapes=[
            pltpu.VMEM(populations.shape, F32),
            pltpu.VMEM((3, verts), F32),
            pltpu.SemaphoreType.DMA((2, 1 + len(PIECES))),
        ],
        compiler_params=pltpu.CompilerParams(vmem_limit_bytes=60 * 1024 * 1024),
    )(*results)


def solution(mesh):
    placed = (
        P(None, ("gx", "gy", "gz")),
        P(None, ("gx", "gy", "gz")),
        P(("gx", "gy", "gz")),
        P(("gx", "gy", "gz"), None),
        P(("gx", "gy", "gz")),
        P(None, "gx", "gy", "gz"),
        P("gx", "gy", "gz"),
        P("gx", "gy", "gz"),
        P(),
    )
    sizes = tuple(mesh.shape[axis] for axis in ("gx", "gy", "gz"))
    return jax.shard_map(
        functools.partial(on_device, sizes),
        mesh=mesh,
        in_specs=placed,
        out_specs=(P(None, "gx", "gy", "gz"), P(None, ("gx", "gy", "gz"))),
        check_vma=False,
    )
```

time: 58.7 us -> 45.8 us (0.78)
  local copies, waits for them, and re-layouts: 8.87 us -> 0 us
  Pallas kernels: 48.7 us -> 44.5 us
    unnamed x20 -> x0, local copies, waits for them, and re-layouts: 8.87 us -> none
    pallas_call x1, Pallas kernels: 48.7 us -> 42.4 us  [on_device(): pl.pallas_call(functools.partial(kernel, sizes), out_shape=(jax.ShapeDtyp...]
    pallas_call x0 -> x1, Pallas kernels: none -> 2.11 us  [on_device(): pl.pallas_call(hand_over, out_shape=[jax.ShapeDtypeStruct(result.shape, F...]
where the time goes in v2:
time: 45.8 us; the launch traced here: 45.2 us
  Pallas kernels  44.5 us (97%)
  between operations  0.64 us (1%)
    pallas_call x1, Pallas kernels, on_device(): pl.pallas_call(functools.partial(kernel, sizes), out_shape=(jax.ShapeDtyp...  42.4 us
    pallas_call x1, Pallas kernels, on_device(): pl.pallas_call(hand_over, out_shape=[jax.ShapeDtypeStruct(result.shape, F...  2.11 us

profile of v2, /device:TPU:1, one launch (start us, length us, event | category | flops | bytes accessed | tf_op | source)
XLA Modules:
  0.0 45.2 jit_solution(14647276562459956631)
XLA Ops:
  0.6 42.4 %shard_map.104 = (f32[19,8,16,128]{3,2,1,0:T(8,128)}, f32[3,2048]{1,0:T(4,128)}) custom-call(f32[3,2048]{1,0:T(4,128)} %off_hbm.1, f32[3,2048]{1,0:T(4,128)} %anc_hbm.1, f32[1,2048]{1,0:T(1,128)} %bitcast.3, s32[1,2048]{1,0:T(1,128)} %bitcast.4, s32[1,2048]{1,0:T(1,128)} %bitcast.5, f32[4]{0:T(128)} %tau_hbm.1, f32[19,8,16,128]{3,2,1,0:T(8,128)} %pop_hbm.1, ...), custom_call_target="tpu_custom_call" | custom-call | tf_op jit(solution)/shard_map/pallas_call | solution.py:595
  43.1 2.1 %shard_map.105 = (f32[19,8,16,128]{3,2,1,0:T(8,128)}, f32[3,2048]{1,0:T(4,128)}) custom-call(f32[19,8,16,128]{3,2,1,0:T(8,128)} %get-tuple-element.4.new_hbm, f32[3,2048]{1,0:T(4,128)} %get-tuple-element.5.vel_hbm), custom_call_target="tpu_custom_call" | custom-call | tf_op jit(solution)/shard_map/pallas_call | solution.py:663

commit v3 on v2

--- a/solution.py
+++ b/solution.py
@@ -14,7 +14,7 @@
 TZ = 32
 WIDE = 4
 PIECES = [pl.ds(start, min(5, 19 - start)) for start in range(0, 19, 5)]
-PARTS = (8, 8, 8, 4, 4)
+PART = 8
 XPAD, YPAD = BX + 2, 32
 F32, BF16, I32 = jnp.float32, jnp.bfloat16, jnp.int32
 
@@ -124,7 +124,9 @@
     cls_hbm,
     flu_hbm,
     out_hbm,
-    vel_ref,
+    ret_hbm,
+    rank_hbm,
+    rel_hbm,
     off_ref,
     anc_ref,
     stf_ref,
@@ -134,6 +136,8 @@
     pops,
     cls,
     flu,
+    rank_ref,
+    rel_ref,
     rows,
     rt,
     lhs,
@@ -160,7 +164,6 @@
     ubuf,
     newp,
     vbuf,
-    ret,
     in_sem,
     out_sem,
     fwd_send,
@@ -200,22 +203,18 @@
         key=lambda at: (min(at[0], n_gy - at[0]) + min(at[1], n_gz - at[1]), at),
     )
     loads = [pltpu.make_async_copy(src, dst, in_sem.at[k]) for k, (src, dst) in enumerate(arguments)]
-    for copy in loads:
-        copy.start()
-
     barrier = pltpu.get_barrier_semaphore()
 
-    @pl.loop(1, groups)
-    def _(d):
-        pl.semaphore_signal(
-            barrier, inc=1, device_id=device(0, d // n_gz, lax.rem(d, n_gz)), device_id_type=MESH
-        )
-
+    for offset in ring[:0:-1]:
+        pl.semaphore_signal(barrier, inc=1, device_id=device(0, *offset), device_id_type=MESH)
     others = [(sx, 0, 0) for sx in (1, -1)]
     others += [(sx, sy, 0) for sx in (1, -1) for sy in (1, -1)]
     others += [(sx, 0, sz) for sx in (1, -1) for sz in (1, -1)]
     for offset in others:
         pl.semaphore_signal(barrier, inc=1, device_id=device(*offset), device_id_type=MESH)
+
+    for copy in loads:
+        copy.start()
 
     loads[0].wait()
     target = tgt_ref[...]
@@ -238,6 +237,14 @@
         )
         base = base + part[:, 128:]
         rt[:, c * 128 : (c + 1) * 128] = jnp.where(rank == slot_id, 1.0, 0.0).astype(BF16)
+        rank_ref[:, c * 128 : (c + 1) * 128] = rank
+    rel_ref[...] = rel
+    kept = [
+        pltpu.make_async_copy(rank_ref, rank_hbm, out_sem.at[1]),
+        pltpu.make_async_copy(rel_ref, rel_hbm, out_sem.at[2]),
+    ]
+    for copy in kept:
+        copy.start()
 
     def high(value):
         return value.astype(BF16).astype(F32)
@@ -281,7 +288,7 @@
             device_id_type=MESH,
         )
 
-    for k in range(groups - 1, 0, -1):
+    for k in range(1, groups):
         forward(k, *ring[k]).start()
 
     wide = 128 * WIDE
@@ -294,8 +301,9 @@
         top = value.astype(BF16)
         return top, (value - top.astype(F32)).astype(BF16)
 
-    def spread(at):
-        blk = jnp.concatenate([inbuf[at * WIDE + e] for e in range(WIDE)], axis=1)
+    def spread(part, at):
+        first = part * PART + at * WIDE
+        blk = jnp.concatenate([inbuf[first + e] for e in range(WIDE)], axis=1)
         tile = blk[6:7].astype(I32)
         tile_x, tile_y, tile_z = tile // 32, lax.rem(tile // 4, 8), lax.rem(tile, 4)
         dist_x = 2.0 * blk[0:1] - lax.rem(x_id, 2).astype(F32)
@@ -303,40 +311,32 @@
         dist_y = 2.0 * blk[1:2] - lax.rem(y_id, 2).astype(F32)
         wy = jnp.where(y_id // 2 == tile_y, jnp.maximum(0.0, 1.0 - jnp.abs(dist_y) * third), 0.0)
         weight = jnp.maximum(0.0, 1.0 - jnp.abs(16.0 * blk[2:3] - z_half))
-        lanes = pl.ds(pl.multiple_of(at * wide, wide), wide)
-        wz[:, lanes] = weight
+        lanes = slice(at * wide, (at + 1) * wide)
+        wz[part][:, lanes] = weight
         for x in range(BX):
-            for part, value in enumerate(split(wx[x : x + 1] * wy)):
-                row = part * SITES + x * BY
-                wxy[row : row + BY, lanes] = value
+            for piece, value in enumerate(split(wx[x : x + 1] * wy)):
+                row = piece * SITES + x * BY
+                wxy[part][row : row + BY, lanes] = value
         for c in range(3):
-            for part, value in enumerate(split(weight * blk[3 + c : 4 + c])):
+            for piece, value in enumerate(split(weight * blk[3 + c : 4 + c])):
                 for z in range(BZ // TZ):
-                    row = (part * 3 + c) * BZ + z * TZ
-                    load[row : row + TZ, lanes] = jnp.where(
+                    row = (piece * 3 + c) * BZ + z * TZ
+                    load[part][row : row + TZ, lanes] = jnp.where(
                         jnp.broadcast_to(tile_z == z, (TZ, wide)), value, jnp.zeros_like(value)
                     )
 
-    first_slot = 0
-    for count in PARTS:
-
-        @pl.loop(max(first_slot, 1), first_slot + count)
-        def _(k):
+    for part in range(groups // PART):
+        for k in range(max(part * PART, 1), (part + 1) * PART):
             forward(k).wait_recv()
-
-        @pl.loop(first_slot // WIDE, (first_slot + count) // WIDE)
-        def _(at):
-            spread(at)
-
-        span = slice(first_slot * 128, (first_slot + count) * 128)
+        for at in range(PART // WIDE):
+            spread(part, at)
         product = lax.dot_general(
-            wxy[:, span], load[:, span], (((1,), (1,)), ((), ())), preferred_element_type=F32
-        )
-        if first_slot == 0:
+            wxy[part][...], load[part][...], (((1,), (1,)), ((), ())), preferred_element_type=F32
+        )
+        if part == 0:
             acc[...] = product
         else:
             acc[...] += product
-        first_slot += count
     for c in range(3):
         here, there = slice(c * BZ, (c + 1) * BZ), slice((3 + c) * BZ, (4 + c) * BZ)
         force[c * SITES : (c + 1) * SITES, :] = (acc[0:SITES, here] + acc[0:SITES, there]) + (
@@ -495,7 +495,7 @@
                 start = c * SITES + x * BY + 8 * h
                 ubuf[start : start + 8, :] = flow[c]
 
-    store = pltpu.make_async_copy(newp, out_hbm, out_sem)
+    store = pltpu.make_async_copy(newp, out_hbm, out_sem.at[0])
     store.start()
 
     turned = [[], []]
@@ -508,7 +508,7 @@
     def backward(k, dy=0, dz=1):
         return pltpu.make_async_remote_copy(
             src_ref=vbuf.at[k],
-            dst_ref=ret.at[dy * n_gz + dz],
+            dst_ref=ret_hbm.at[dy * n_gz + dz],
             send_sem=back_send.at[k],
             recv_sem=back_recv.at[k],
             device_id=device(0, -dy, -dz),
@@ -516,12 +516,13 @@
         )
 
     for pair in range(groups // 2 - 1, -1, -1):
-        lanes = slice(pair * 256, (pair + 1) * 256)
-        block = wxy[:, lanes]
+        part, start = 2 * pair // PART, 2 * pair % PART * 128
+        lanes = slice(start, start + 256)
+        block = wxy[part][:, lanes]
         picked = jnp.dot(
             flow_all, jnp.concatenate([block, block], axis=0), preferred_element_type=F32
         )
-        weight = wz[:, lanes]
+        weight = wz[part][:, lanes]
         tile = jnp.concatenate([inbuf[2 * pair + e, 6:7, :] for e in range(2)], axis=1)
         tile_z = jnp.broadcast_to(lax.rem(tile.astype(I32), 4), (TZ, 256))
         for c in range(3):
@@ -537,41 +538,71 @@
                 backward(k, *ring[k]).start()
 
     halo_sent(sent)
-    ret[0] = vbuf[0]
+    mine = pltpu.make_async_copy(vbuf.at[0], ret_hbm.at[0], out_sem.at[3])
+    mine.start()
+    for copy in kept:
+        copy.wait()
+    store.wait()
 
     @pl.loop(1, groups)
     def _(k):
         backward(k).wait_recv()
 
-    answer = jnp.concatenate([ret[:, c, :] for c in range(3)], axis=0)
+    @pl.loop(1, groups)
+    def _(k):
+        backward(k).wait_send()
+
+    mine.wait()
+
+
+def hand_over(
+    new_hbm,
+    ret_hbm,
+    rank_hbm,
+    rel_hbm,
+    new_out,
+    vel_out,
+    new_ref,
+    ret_ref,
+    rank_ref,
+    rel_ref,
+    vel_ref,
+    in_sem,
+    out_sem,
+):
+    groups, verts = ret_ref.shape[0], rank_ref.shape[1]
+    answers = [(rank_hbm, rank_ref), (rel_hbm, rel_ref), (ret_hbm, ret_ref)]
+    answers = [pltpu.make_async_copy(src, dst, in_sem.at[k]) for k, (src, dst) in enumerate(answers)]
+    inward = [
+        pltpu.make_async_copy(new_hbm.at[part], new_ref.at[part], in_sem.at[3 + k])
+        for k, part in enumerate(PIECES)
+    ]
+    outward = [
+        pltpu.make_async_copy(new_ref.at[part], new_out.at[part], out_sem.at[k])
+        for k, part in enumerate(PIECES)
+    ]
+    for copy in answers + inward:
+        copy.start()
+    answers[0].wait()
+    slot_id = lax.broadcasted_iota(I32, (CAP, verts), 0).astype(F32)
+    slots = jnp.where(rank_ref[...] == slot_id, 1.0, 0.0).astype(BF16)
+    for copy in answers[1:]:
+        copy.wait()
+    answer = jnp.concatenate([ret_ref[:, c, :] for c in range(3)], axis=0)
     answer_hi = answer.astype(BF16)
     answer_lo = (answer - answer_hi.astype(F32)).astype(BF16)
-    found = jnp.dot(
-        jnp.concatenate([answer_hi, answer_lo], axis=0), rt[...], preferred_element_type=F32
-    )
-    found = found[0 : 3 * groups] + found[3 * groups :]
+    both = jnp.concatenate([answer_hi, answer_lo], axis=1)
+    found = jnp.dot(both, jnp.concatenate([slots, slots], axis=0), preferred_element_type=F32)
+    for k, copy in enumerate(inward):
+        copy.wait()
+        outward[k].start()
+    member = rel_ref[...] == lax.broadcasted_iota(I32, (groups, verts), 0)
     for c in range(3):
         vel_ref[c : c + 1, :] = jnp.sum(
             jnp.where(member, found[c * groups : (c + 1) * groups], 0.0), axis=0, keepdims=True
         )
-
-    @pl.loop(1, groups)
-    def _(k):
-        backward(k).wait_send()
-
-    store.wait()
-
-
-def hand_over(new_hbm, vel_hbm, new_out, vel_out, new_ref, vel_ref, sems):
-    hops = [(vel_hbm, vel_ref, vel_out)]
-    hops += [(new_hbm.at[part], new_ref.at[part], new_out.at[part]) for part in PIECES]
-    inward = [pltpu.make_async_copy(src, mid, sems.at[0, k]) for k, (src, mid, _) in enumerate(hops)]
-    outward = [pltpu.make_async_copy(mid, dst, sems.at[1, k]) for k, (_, mid, dst) in enumerate(hops)]
-    for copy in inward:
-        copy.start()
-    for k, copy in enumerate(inward):
-        copy.wait()
-        outward[k].start()
+    outward.append(pltpu.make_async_copy(vel_ref, vel_out, out_sem.at[len(PIECES)]))
+    outward[-1].start()
     for copy in outward:
         copy.wait()
 
@@ -590,16 +621,17 @@
 ):
     groups = sizes[1] * sizes[2]
     verts = offsets.shape[1]
-    vmem = pl.BlockSpec(memory_space=pltpu.VMEM)
     hbm = pl.BlockSpec(memory_space=pltpu.HBM)
     results = pl.pallas_call(
         functools.partial(kernel, sizes),
         out_shape=(
             jax.ShapeDtypeStruct(populations.shape, F32),
-            jax.ShapeDtypeStruct((3, verts), F32),
+            jax.ShapeDtypeStruct((groups, 4, CAP), F32),
+            jax.ShapeDtypeStruct((1, verts), F32),
+            jax.ShapeDtypeStruct((1, verts), I32),
         ),
         in_specs=[hbm] * 9,
-        out_specs=(hbm, vmem),
+        out_specs=[hbm] * 4,
         scratch_shapes=[
             pltpu.VMEM((3, verts), F32),
             pltpu.VMEM((3, verts), F32),
@@ -610,14 +642,16 @@
             pltpu.VMEM((19, BX, BY, BZ), F32),
             pltpu.VMEM((BX, BY, BZ), I32),
             pltpu.VMEM((BX, BY, BZ), I32),
+            pltpu.VMEM((1, verts), F32),
+            pltpu.VMEM((1, verts), I32),
             pltpu.VMEM((16, verts), F32),
             pltpu.VMEM((CAP, verts), BF16),
             pltpu.VMEM((groups * 16, verts), BF16),
             pltpu.VMEM((groups, 8, CAP), F32),
             pltpu.VMEM((groups, 8, CAP), F32),
-            pltpu.VMEM((TZ, groups * CAP), F32),
-            pltpu.VMEM((2 * SITES, groups * CAP), BF16),
-            pltpu.VMEM((6 * BZ, groups * CAP), BF16),
+            [pltpu.VMEM((TZ, PART * CAP), F32)] * (groups // PART),
+            [pltpu.VMEM((2 * SITES, PART * CAP), BF16)] * (groups // PART),
+            [pltpu.VMEM((6 * BZ, PART * CAP), BF16)] * (groups // PART),
             pltpu.VMEM((2 * SITES, 6 * BZ), F32),
             pltpu.VMEM((3 * SITES, BZ), F32),
             pltpu.VMEM((19 * XPAD * YPAD, BZ), F32),
@@ -636,9 +670,8 @@
             pltpu.VMEM((3 * SITES, BZ), F32),
             pltpu.VMEM((19, BX, BY, BZ), F32),
             pltpu.VMEM((groups, 4, CAP), F32),
-            pltpu.VMEM((groups, 4, CAP), F32),
             pltpu.SemaphoreType.DMA((9,)),
-            pltpu.SemaphoreType.DMA,
+            pltpu.SemaphoreType.DMA((4,)),
             pltpu.SemaphoreType.DMA((groups,)),
             pltpu.SemaphoreType.DMA((groups,)),
             pltpu.SemaphoreType.DMA((2, 18)),
@@ -662,13 +695,20 @@
     )
     return pl.pallas_call(
         hand_over,
-        out_shape=[jax.ShapeDtypeStruct(result.shape, F32) for result in results],
-        in_specs=[hbm] * 2,
+        out_shape=[
+            jax.ShapeDtypeStruct(populations.shape, F32),
+            jax.ShapeDtypeStruct((3, verts), F32),
+        ],
+        in_specs=[hbm] * 4,
         out_specs=[hbm] * 2,
         scratch_shapes=[
             pltpu.VMEM(populations.shape, F32),
+            pltpu.VMEM((groups, 4, CAP), F32),
+            pltpu.VMEM((1, verts), F32),
+            pltpu.VMEM((1, verts), I32),
             pltpu.VMEM((3, verts), F32),
-            pltpu.SemaphoreType.DMA((2, 1 + len(PIECES))),
+            pltpu.SemaphoreType.DMA((3 + len(PIECES),)),
+            pltpu.SemaphoreType.DMA((len(PIECES) + 1,)),
         ],
         compiler_params=pltpu.CompilerParams(vmem_limit_bytes=60 * 1024 * 1024),
     )(*results)

time: 45.8 us -> 43.1 us (0.941)
  Pallas kernels: 44.5 us -> 42.2 us
    pallas_call x1, Pallas kernels: 42.4 us -> 39.9 us  [on_device(): pl.pallas_call(functools.partial(kernel, sizes), out_shape=(jax.ShapeDtyp...]
where the time goes in v3:
time: 43.1 us; the launch traced here: 42.9 us
  Pallas kernels  42.2 us (98%)
  between operations  0.64 us (1%)
    pallas_call x1, Pallas kernels, on_device(): pl.pallas_call(functools.partial(kernel, sizes), out_shape=(jax.ShapeDtyp...  39.9 us
    pallas_call x1, Pallas kernels, on_device(): pl.pallas_call(hand_over, out_shape=[jax.ShapeDtypeStruct(populations.sha...  2.32 us

profile of v3, /device:TPU:1, one launch (start us, length us, event | category | flops | bytes accessed | tf_op | source)
XLA Modules:
  0.0 42.9 jit_solution(8623978043330106670)
XLA Ops:
  0.6 39.9 %shard_map.104 = (f32[19,8,16,128]{3,2,1,0:T(8,128)}, f32[32,4,128]{2,1,0:T(4,128)}, f32[1,2048]{1,0:T(1,128)}, s32[1,2048]{1,0:T(1,128)}) custom-call(f32[3,2048]{1,0:T(4,128)} %off_hbm.1, f32[3,2048]{1,0:T(4,128)} %anc_hbm.1, f32[1,2048]{1,0:T(1,128)} %bitcast.3, s32[1,2048]{1,0:T(1,128)} %bitcast.4, s32[1,2048]{1,0:T(1,128)} %bitcast.5, f32[4]{0:T(128)} %tau_hbm.1, ...), custom_call_target="tpu_custom_call" | custom-call | tf_op jit(solution)/shard_map/pallas_call | solution.py:625
  40.6 2.3 %shard_map.105 = (f32[19,8,16,128]{3,2,1,0:T(8,128)}, f32[3,2048]{1,0:T(4,128)}) custom-call(f32[19,8,16,128]{3,2,1,0:T(8,128)} %get-tuple-element.6.new_hbm, f32[32,4,128]{2,1,0:T(4,128)} %get-tuple-element.7.ret_hbm, f32[1,2048]{1,0:T(1,128)} %get-tuple-element.8.rank_hbm, s32[1,2048]{1,0:T(1,128)} %get-tuple-element.9.rel_hbm), custom_call_target="tpu_custom_call" | custom-call | tf_op jit(solution)/shard_map/pallas_call | solution.py:696

commit v4 on v3

--- a/solution.py
+++ b/solution.py
@@ -14,7 +14,7 @@
 TZ = 32
 WIDE = 4
 PIECES = [pl.ds(start, min(5, 19 - start)) for start in range(0, 19, 5)]
-PART = 8
+PARTS = (8, 8, 8, 4, 4)
 XPAD, YPAD = BX + 2, 32
 F32, BF16, I32 = jnp.float32, jnp.bfloat16, jnp.int32
 
@@ -50,15 +50,20 @@
 
 XSET = [crossing(0, 1), crossing(0, -1)]
 YSET = [crossing(1, 1), crossing(1, -1)]
-ZSET = [crossing(2, 1), crossing(2, -1)]
 
 
 def dist_of(*velocity):
     return lattice_velocity.index(tuple(velocity))
 
 
-def z_lane(side, index, x):
-    return ZSET[side].index(index) * XPAD + x + 1
+ZPAIRS = [
+    (dist_of(cx, cy, 1), dist_of(cx, cy, -1))
+    for cx, cy in ((0, 0), (1, 0), (-1, 0), (0, 1), (0, -1))
+]
+
+
+def z_lane(q, x):
+    return 2 * (q * XPAD + x + 1)
 
 
 def row_of(index, x, y):
@@ -77,6 +82,58 @@
     return density, flow
 
 
+def prepare(f, omega, fluid):
+    density = functools.reduce(lambda a, b: a + b, f)
+    keep = 1.0 - omega
+    kept = [None] * 19
+    kept[0] = jnp.where(fluid, keep * f[0], f[0])
+    for i, j in pairs:
+        kept[i] = jnp.where(fluid, keep * f[i], f[j])
+        kept[j] = jnp.where(fluid, keep * f[j], f[i])
+    momentum = []
+    for axis in range(3):
+        plus = [f[i] for i in crossing(axis, 1)]
+        minus = [f[i] for i in crossing(axis, -1)]
+        momentum.append(functools.reduce(lambda a, b: a + b, plus) - functools.reduce(lambda a, b: a + b, minus))
+    amount = jnp.where(fluid, omega * density, 0.0)
+    gain = jnp.where(fluid, 1.0 - 0.5 * omega, 0.0)
+    return kept, [1.0 / density, *momentum, amount, gain]
+
+
+def complete(kept, values, force):
+    inverse, amount, gain = values[0], values[4], values[5]
+    flow = [(values[1 + a] + 0.5 * force[a]) * inverse for a in range(3)]
+    speed_sq = flow[0] * flow[0] + flow[1] * flow[1] + flow[2] * flow[2]
+    work = flow[0] * force[0] + flow[1] * force[1] + flow[2] * force[2]
+    base = amount * (1.0 - 1.5 * speed_sq) - (3.0 * gain) * work
+    added = added_terms(base, flow, [amount * flow[a] for a in range(3)], [gain * force[a] for a in range(3)])
+    return [kept[i] + added[i] for i in range(19)]
+
+
+def added_terms(base, flow, momentum, push):
+    steep = [4.5 * momentum[a] + 9.0 * push[a] for a in range(3)]
+    slope = [3.0 * (momentum[a] + push[a]) for a in range(3)]
+    added = [lattice_weight[0] * base] + [None] * 18
+
+    def along(values, velocity):
+        total = None
+        for axis in range(3):
+            if velocity[axis]:
+                if total is None:
+                    total = values[axis] if velocity[axis] > 0 else -values[axis]
+                else:
+                    total = total + values[axis] if velocity[axis] > 0 else total - values[axis]
+        return total
+
+    for i, j in pairs:
+        velocity = lattice_velocity[i]
+        even = base + along(flow, velocity) * along(steep, velocity)
+        odd = along(slope, velocity)
+        added[i] = lattice_weight[i] * (even + odd)
+        added[j] = lattice_weight[i] * (even - odd)
+    return added
+
+
 def collide(f, force, omega, fluid):
     density, flow = moments(f, force)
     speed_sq = flow[0] * flow[0] + flow[1] * flow[1] + flow[2] * flow[2]
@@ -87,28 +144,11 @@
     base = amount * (1.0 - 1.5 * speed_sq) - (3.0 * gain) * work
     momentum = [amount * flow[a] for a in range(3)]
     push = [gain * force[a] for a in range(3)]
-    steep = [4.5 * momentum[a] + 9.0 * push[a] for a in range(3)]
-    slope = [3.0 * (momentum[a] + push[a]) for a in range(3)]
-    result = [None] * 19
-    result[0] = jnp.where(fluid, keep * f[0] + lattice_weight[0] * base, f[0])
-
-    def along(values, velocity):
-        total = None
-        for axis in range(3):
-            if velocity[axis]:
-                if total is None:
-                    total = values[axis] if velocity[axis] > 0 else -values[axis]
-                else:
-                    total = total + values[axis] if velocity[axis] > 0 else total - values[axis]
-        return total
-
+    added = added_terms(base, flow, momentum, push)
+    result = [jnp.where(fluid, keep * f[0] + added[0], f[0])] + [None] * 18
     for i, j in pairs:
-        velocity = lattice_velocity[i]
-        even = base + along(flow, velocity) * along(steep, velocity)
-        odd = along(slope, velocity)
-        weight = lattice_weight[i]
-        result[i] = jnp.where(fluid, keep * f[i] + weight * (even + odd), f[j])
-        result[j] = jnp.where(fluid, keep * f[j] + weight * (even - odd), f[i])
+        result[i] = jnp.where(fluid, keep * f[i] + added[i], f[j])
+        result[j] = jnp.where(fluid, keep * f[j] + added[j], f[i])
     return result
 
 
@@ -163,6 +203,7 @@
     zp,
     ubuf,
     newp,
+    calm,
     vbuf,
     in_sem,
     out_sem,
@@ -291,6 +332,29 @@
     for k in range(1, groups):
         forward(k, *ring[k]).start()
 
+    for copy in loads[5:]:
+        copy.wait()
+
+    taus = [1.0 / jnp.full((8, 128), tau_ref[k], F32) for k in range(4)]
+
+    def site_values(x, h):
+        rows_at = slice(8 * h, 8 * h + 8)
+        klass = cls[x, rows_at, :]
+        omega = jnp.where(
+            klass < 2, jnp.where(klass == 0, taus[0], taus[1]), jnp.where(klass == 2, taus[2], taus[3])
+        )
+        return omega, flu[x, rows_at, :] > 0
+
+    for x in range(BX):
+        for h in range(2):
+            rows_here = slice(8 * h, 8 * h + 8)
+            omega, fluid = site_values(x, h)
+            still, values = prepare([pops[i, x, rows_here, :] for i in range(19)], omega, fluid)
+            for i in range(19):
+                calm[i, x, rows_here, :] = still[i]
+            for k in range(6):
+                calm[19 + k, x, rows_here, :] = values[k]
+
     wide = 128 * WIDE
     x_id = lax.broadcasted_iota(I32, (BX, wide), 0)
     y_id = lax.broadcasted_iota(I32, (BY, wide), 0)
@@ -302,7 +366,7 @@
         return top, (value - top.astype(F32)).astype(BF16)
 
     def spread(part, at):
-        first = part * PART + at * WIDE
+        first = sum(PARTS[:part]) + at * WIDE
         blk = jnp.concatenate([inbuf[first + e] for e in range(WIDE)], axis=1)
         tile = blk[6:7].astype(I32)
         tile_x, tile_y, tile_z = tile // 32, lax.rem(tile // 4, 8), lax.rem(tile, 4)
@@ -325,10 +389,11 @@
                         jnp.broadcast_to(tile_z == z, (TZ, wide)), value, jnp.zeros_like(value)
                     )
 
-    for part in range(groups // PART):
-        for k in range(max(part * PART, 1), (part + 1) * PART):
+    for part, count in enumerate(PARTS):
+        start = sum(PARTS[:part])
+        for k in range(max(start, 1), start + count):
             forward(k).wait_recv()
-        for at in range(PART // WIDE):
+        for at in range(count // WIDE):
             spread(part, at)
         product = lax.dot_general(
             wxy[part][...], load[part][...], (((1,), (1,)), ((), ())), preferred_element_type=F32
@@ -343,19 +408,6 @@
             acc[SITES:, here] + acc[SITES:, there]
         )
 
-    for copy in loads[5:]:
-        copy.wait()
-
-    taus = [1.0 / jnp.full((8, 128), tau_ref[k], F32) for k in range(4)]
-
-    def site_values(x, h):
-        rows_at = slice(8 * h, 8 * h + 8)
-        klass = cls[x, rows_at, :]
-        omega = jnp.where(
-            klass < 2, jnp.where(klass == 0, taus[0], taus[1]), jnp.where(klass == 2, taus[2], taus[3])
-        )
-        return omega, flu[x, rows_at, :] > 0
-
     def forces(x, h):
         starts = [c * SITES + x * BY + 8 * h for c in range(3)]
         return [force[start : start + 8, :] for start in starts]
@@ -365,13 +417,13 @@
         for s, sign in enumerate((1, -1)):
             early.append(((sign, 0, 0), xs.at[p, s], xr.at[p, s]))
             late.append(((0, sign, 0), ys.at[p, s], yr.at[p, s]))
-            late.append(((0, 0, sign), zs.at[p, s], zr.at[p, s]))
+            late.append(((0, 0, sign), zs.at[p], zr.at[p, s]))
             for t, other in enumerate((1, -1)):
                 edge = pl.ds(8 if other > 0 else 0, 8)
                 spot = XSET[s].index(dist_of(sign, other, 0))
                 early.append(((sign, other, 0), xs.at[p, s, spot, edge], xyr.at[p, s, t]))
-                early.append(((other, 0, sign), ze.at[p, s], xzr.at[p, s, t]))
-                late.append(((0, other, sign), zs.at[p, s, edge], yzr.at[p, s, t]))
+                early.append(((other, 0, sign), ze.at[p], xzr.at[p, s, t]))
+                late.append(((0, other, sign), zs.at[p, edge], yzr.at[p, s, t]))
         hops = lambda message: -sum(abs(v) for v in message[0])
         return sorted(early, key=hops), sorted(late, key=hops)
 
@@ -394,45 +446,37 @@
         for i in range(19):
             cx, cy, cz = lattice_velocity[i]
             start = row_of(i, x - cx, 8 * h - cy)
-            value = field[p][start : start + 8, :]
-            if cz:
-                s = 0 if cz > 0 else 1
-                border = zp[p, s, 8 + 8 * h - cy : 16 + 8 * h - cy, :]
-                lane = z_lane(s, i, x - cx)
-                edge = 0 if cz > 0 else 127
-                shift = 128 - lane if cz > 0 else 127 - lane
-                value = jnp.where(
-                    lane8 == edge,
-                    pltpu.roll(border, shift, axis=1),
-                    pltpu.roll(value, 1 if cz > 0 else 127, axis=1),
-                )
-            found.append(value)
+            found.append(field[p][start : start + 8, :])
+        for q, (up, down) in enumerate(ZPAIRS):
+            cx, cy, _ = lattice_velocity[up]
+            border = zp[p, 8 + 8 * h - cy : 16 + 8 * h - cy, :]
+            border = pltpu.roll(border, 127 - z_lane(q, x - cx), axis=1)
+            found[up] = jnp.where(lane8 == 0, border, pltpu.roll(found[up], 1, axis=1))
+            found[down] = jnp.where(lane8 == 127, border, pltpu.roll(found[down], 127, axis=1))
         return found
 
-    def sweep(p, source, earlier):
+    def sweep(p, source, rule, earlier):
         def plane(x, borders):
             incoming = [source(x, h) for h in range(2)]
             for h in range(2):
-                omega, fluid = site_values(x, h)
-                result = collide(incoming[h], forces(x, h), omega, fluid)
+                result = rule(incoming[h], x, h)
                 for i in range(19):
                     start = row_of(i, x, 8 * h)
                     field[p][start : start + 8, :] = result[i]
-                for s in range(2):
-                    for i in ZSET[s]:
-                        lane = z_lane(s, i, x)
-                        shift = lane + 1 if s == 0 else lane
-                        borders[2 * s + h] = jnp.where(
-                            lane8 == lane, pltpu.roll(result[i], shift, axis=1), borders[2 * s + h]
-                        )
+                for q, (up, down) in enumerate(ZPAIRS):
+                    lane = z_lane(q, x)
+                    both = jnp.where(lane8 == 0, result[down], result[up])
+                    borders[h] = jnp.where(
+                        lane8 // 2 == lane // 2, pltpu.roll(both, lane + 1, axis=1), borders[h]
+                    )
 
         copies, early = halo(p)
-        borders = [jnp.zeros((8, 128), F32)] * 4
+        borders = [jnp.zeros((8, 128), F32)] * 2
         for x in (0, BX - 1):
             plane(x, borders)
+        for h in range(2):
+            ze[p, 8 * h : 8 * h + 8, :] = borders[h]
         for s in range(2):
-            for h in range(2):
-                ze[p, s, 8 * h : 8 * h + 8, :] = borders[2 * s + h]
             for k, i in enumerate(XSET[s]):
                 start = row_of(i, BX - 1 if s == 0 else 0, 0)
                 xs[p, s, k] = field[p][start : start + BY, :]
@@ -440,9 +484,9 @@
             copy.start()
         for x in range(1, BX - 1):
             plane(x, borders)
+        for h in range(2):
+            zs[p, 8 * h : 8 * h + 8, :] = borders[h]
         for s in range(2):
-            for h in range(2):
-                zs[p, s, 8 * h : 8 * h + 8, :] = borders[2 * s + h]
             for k, i in enumerate(YSET[s]):
                 ys[p, s, k] = field[p][pl.ds(row_of(i, 0, BY - 1 if s == 0 else 0), BX, stride=YPAD), :]
         for copy in copies[early:]:
@@ -451,27 +495,34 @@
         for copy in copies:
             copy.wait_recv()
         lane16 = lax.broadcasted_iota(I32, (BY, 128), 1)
+        planes, edges = [], []
         for s, sign in enumerate((1, -1)):
             for k, i in enumerate(XSET[s]):
                 start = row_of(i, -1 if s == 0 else BX, 0)
                 field[p][start : start + BY, :] = xr[p, s, k]
             for k, i in enumerate(YSET[s]):
                 field[p][pl.ds(row_of(i, 0, -1 if s == 0 else BY), BX, stride=YPAD), :] = yr[p, s, k]
-            plane = zr[p, s]
+            plane_in = pltpu.roll(zr[p, s], sign % 128, axis=1)
             for t, other in enumerate((1, -1)):
                 to, row = (-1, 7) if other > 0 else (BY, 0)
                 start = row_of(dist_of(sign, other, 0), -1 if s == 0 else BX, to)
                 field[p][start : start + 1, :] = xyr[p, s, t, row : row + 1, :]
-                zp[p, s, 8 + to : 9 + to, :] = yzr[p, s, t, row : row + 1, :]
-                i = dist_of(other, 0, sign)
-                lane = z_lane(s, i, -1 if other > 0 else BX)
-                shift = 128 - BX if other > 0 else BX
-                plane = jnp.where(lane16 == lane, pltpu.roll(xzr[p, s, t], shift, axis=1), plane)
-            zp[p, s, 8:24, :] = plane
+                edges.append(pltpu.roll(yzr[p, s, t], sign % 128, axis=1)[row : row + 1])
+                q = [lattice_velocity[up][0] for up, _ in ZPAIRS].index(other)
+                lane = z_lane(q, -1 if other > 0 else BX)
+                shift = (sign - 2 * BX * other) % 128
+                plane_in = jnp.where(
+                    lane16 // 2 == lane // 2, pltpu.roll(xzr[p, s, t], shift, axis=1), plane_in
+                )
+            planes.append(plane_in)
+        zp[p, 8:24, :] = jnp.where(lane16 % 2 == 1, planes[0], planes[1])
+        odd = lane16[0:1] % 2 == 1
+        zp[p, 7:8, :] = jnp.where(odd, edges[0], edges[2])
+        zp[p, 24:25, :] = jnp.where(odd, edges[1], edges[3])
         return copies
 
     def first(x, h):
-        return [pops[i, x, 8 * h : 8 * h + 8, :] for i in range(19)]
+        return [calm[i, x, 8 * h : 8 * h + 8, :] for i in range(25)]
 
     def forward_sent():
         @pl.loop(1, groups)
@@ -482,8 +533,15 @@
         for copy in copies:
             copy.wait_send()
 
-    sent = sweep(0, first, forward_sent)
-    sent = sweep(1, functools.partial(streamed, 0), functools.partial(halo_sent, sent))
+    def second_rule(incoming, x, h):
+        omega, fluid = site_values(x, h)
+        return collide(incoming, forces(x, h), omega, fluid)
+
+    def first_rule(incoming, x, h):
+        return complete(incoming[:19], incoming[19:], forces(x, h))
+
+    sent = sweep(0, first, first_rule, forward_sent)
+    sent = sweep(1, functools.partial(streamed, 0), second_rule, functools.partial(halo_sent, sent))
 
     for x in range(BX):
         incoming = [streamed(1, x, h) for h in range(2)]
@@ -516,7 +574,8 @@
         )
 
     for pair in range(groups // 2 - 1, -1, -1):
-        part, start = 2 * pair // PART, 2 * pair % PART * 128
+        part = max(p for p in range(len(PARTS)) if sum(PARTS[:p]) <= 2 * pair)
+        start = (2 * pair - sum(PARTS[:part])) * 128
         lanes = slice(start, start + 256)
         block = wxy[part][:, lanes]
         picked = jnp.dot(
@@ -649,9 +708,9 @@
             pltpu.VMEM((groups * 16, verts), BF16),
             pltpu.VMEM((groups, 8, CAP), F32),
             pltpu.VMEM((groups, 8, CAP), F32),
-            [pltpu.VMEM((TZ, PART * CAP), F32)] * (groups // PART),
-            [pltpu.VMEM((2 * SITES, PART * CAP), BF16)] * (groups // PART),
-            [pltpu.VMEM((6 * BZ, PART * CAP), BF16)] * (groups // PART),
+            [pltpu.VMEM((TZ, count * CAP), F32) for count in PARTS],
+            [pltpu.VMEM((2 * SITES, count * CAP), BF16) for count in PARTS],
+            [pltpu.VMEM((6 * BZ, count * CAP), BF16) for count in PARTS],
             pltpu.VMEM((2 * SITES, 6 * BZ), F32),
             pltpu.VMEM((3 * SITES, BZ), F32),
             pltpu.VMEM((19 * XPAD * YPAD, BZ), F32),
@@ -661,14 +720,15 @@
             pltpu.VMEM((2, 2, 5, BX, BZ), F32),
             pltpu.VMEM((2, 2, 5, BX, BZ), F32),
             pltpu.VMEM((2, 2, 2, BX, BZ), F32),
-            pltpu.VMEM((2, 2, BY, 128), F32),
-            pltpu.VMEM((2, 2, BY, 128), F32),
+            pltpu.VMEM((2, BY, 128), F32),
+            pltpu.VMEM((2, BY, 128), F32),
             pltpu.VMEM((2, 2, BY, 128), F32),
             pltpu.VMEM((2, 2, 2, BY, 128), F32),
             pltpu.VMEM((2, 2, 2, 8, 128), F32),
-            pltpu.VMEM((2, 2, YPAD, 128), F32),
+            pltpu.VMEM((2, YPAD, 128), F32),
             pltpu.VMEM((3 * SITES, BZ), F32),
             pltpu.VMEM((19, BX, BY, BZ), F32),
+            pltpu.VMEM((25, BX, BY, BZ), F32),
             pltpu.VMEM((groups, 4, CAP), F32),
             pltpu.SemaphoreType.DMA((9,)),
             pltpu.SemaphoreType.DMA((4,)),

time: 43.1 us -> 42.3 us (0.981)
  Pallas kernels: 42.2 us -> 41.4 us
    pallas_call x1, Pallas kernels: 39.9 us -> 39.1 us  [on_device(): pl.pallas_call(functools.partial(kernel, sizes), out_shape=(jax.ShapeDtyp...]
where the time goes in v4:
time: 42.3 us; the launch traced here: 42 us
  Pallas kernels  41.4 us (98%)
  between operations  0.64 us (2%)
    pallas_call x1, Pallas kernels, on_device(): pl.pallas_call(functools.partial(kernel, sizes), out_shape=(jax.ShapeDtyp...  39.1 us
    pallas_call x1, Pallas kernels, on_device(): pl.pallas_call(hand_over, out_shape=[jax.ShapeDtypeStruct(populations.sha...  2.32 us

profile of v4, /device:TPU:1, one launch (start us, length us, event | category | flops | bytes accessed | tf_op | source)
XLA Modules:
  0.0 42.0 jit_solution(6551934127104255786)
XLA Ops:
  0.6 39.1 %shard_map.104 = (f32[19,8,16,128]{3,2,1,0:T(8,128)}, f32[32,4,128]{2,1,0:T(4,128)}, f32[1,2048]{1,0:T(1,128)}, s32[1,2048]{1,0:T(1,128)}) custom-call(f32[3,2048]{1,0:T(4,128)} %off_hbm.1, f32[3,2048]{1,0:T(4,128)} %anc_hbm.1, f32[1,2048]{1,0:T(1,128)} %bitcast.3, s32[1,2048]{1,0:T(1,128)} %bitcast.4, s32[1,2048]{1,0:T(1,128)} %bitcast.5, f32[4]{0:T(128)} %tau_hbm.1, ...), custom_call_target="tpu_custom_call" | custom-call | tf_op jit(solution)/shard_map/pallas_call | solution.py:684
  39.7 2.3 %shard_map.105 = (f32[19,8,16,128]{3,2,1,0:T(8,128)}, f32[3,2048]{1,0:T(4,128)}) custom-call(f32[19,8,16,128]{3,2,1,0:T(8,128)} %get-tuple-element.6.new_hbm, f32[32,4,128]{2,1,0:T(4,128)} %get-tuple-element.7.ret_hbm, f32[1,2048]{1,0:T(1,128)} %get-tuple-element.8.rank_hbm, s32[1,2048]{1,0:T(1,128)} %get-tuple-element.9.rel_hbm), custom_call_target="tpu_custom_call" | custom-call | tf_op jit(solution)/shard_map/pallas_call | solution.py:756

commit v5 on v4

--- a/solution.py
+++ b/solution.py
@@ -14,7 +14,7 @@
 TZ = 32
 WIDE = 4
 PIECES = [pl.ds(start, min(5, 19 - start)) for start in range(0, 19, 5)]
-PARTS = (8, 8, 8, 4, 4)
+PARTS = (4, 4, 4, 4, 4, 4, 4, 4)
 XPAD, YPAD = BX + 2, 32
 F32, BF16, I32 = jnp.float32, jnp.bfloat16, jnp.int32
 
@@ -540,8 +540,9 @@
     def first_rule(incoming, x, h):
         return complete(incoming[:19], incoming[19:], forces(x, h))
 
-    sent = sweep(0, first, first_rule, forward_sent)
-    sent = sweep(1, functools.partial(streamed, 0), second_rule, functools.partial(halo_sent, sent))
+    sent = sweep(0, first, first_rule, lambda: None)
+    earlier_sent = sent
+    sent = sweep(1, functools.partial(streamed, 0), second_rule, lambda: (forward_sent(), halo_sent(earlier_sent)))
 
     for x in range(BX):
         incoming = [streamed(1, x, h) for h in range(2)]
@@ -605,11 +606,11 @@
 
     @pl.loop(1, groups)
     def _(k):
-        backward(k).wait_recv()
+        backward(k).wait_send()
 
     @pl.loop(1, groups)
     def _(k):
-        backward(k).wait_send()
+        backward(k).wait_recv()
 
     mine.wait()
 

time: 42.3 us -> 42 us (level)
  no operation moved by 1% of the time
where the time goes in v5:
time: 42 us; the launch traced here: 41.8 us
  Pallas kernels  41.2 us (98%)
  between operations  0.64 us (2%)
    pallas_call x1, Pallas kernels, on_device(): pl.pallas_call(functools.partial(kernel, sizes), out_shape=(jax.ShapeDtyp...  38.8 us
    pallas_call x1, Pallas kernels, on_device(): pl.pallas_call(hand_over, out_shape=[jax.ShapeDtypeStruct(populations.sha...  2.32 us

profile of v5, /device:TPU:1, one launch (start us, length us, event | category | flops | bytes accessed | tf_op | source)
XLA Modules:
  0.0 41.8 jit_solution(4760070849373163636)
XLA Ops:
  0.6 38.8 %shard_map.104 = (f32[19,8,16,128]{3,2,1,0:T(8,128)}, f32[32,4,128]{2,1,0:T(4,128)}, f32[1,2048]{1,0:T(1,128)}, s32[1,2048]{1,0:T(1,128)}) custom-call(f32[3,2048]{1,0:T(4,128)} %off_hbm.1, f32[3,2048]{1,0:T(4,128)} %anc_hbm.1, f32[1,2048]{1,0:T(1,128)} %bitcast.3, s32[1,2048]{1,0:T(1,128)} %bitcast.4, s32[1,2048]{1,0:T(1,128)} %bitcast.5, f32[4]{0:T(128)} %tau_hbm.1, ...), custom_call_target="tpu_custom_call" | custom-call | tf_op jit(solution)/shard_map/pallas_call | solution.py:685
  39.5 2.3 %shard_map.105 = (f32[19,8,16,128]{3,2,1,0:T(8,128)}, f32[3,2048]{1,0:T(4,128)}) custom-call(f32[19,8,16,128]{3,2,1,0:T(8,128)} %get-tuple-element.6.new_hbm, f32[32,4,128]{2,1,0:T(4,128)} %get-tuple-element.7.ret_hbm, f32[1,2048]{1,0:T(1,128)} %get-tuple-element.8.rank_hbm, s32[1,2048]{1,0:T(1,128)} %get-tuple-element.9.rel_hbm), custom_call_target="tpu_custom_call" | custom-call | tf_op jit(solution)/shard_map/pallas_call | solution.py:757
